TPU v7x, 32 devices: a whole 2x2x4 slice. The times are simulated.
32 devices in a mesh: groups: 2 (over x), graph: 16 (over z, y, core).
Axes of the slice: x: 2, y: 2, z: 4, core: 2. Of those that a mesh axis runs over, the one named last changes fastest.
Arguments:
- node_irreps: bfloat16 [1536, 49, 128], P(('groups', 'graph')), parts along dimension 0, may hold values from -6 to 6
- cotangent: bfloat16 [1536, 49, 128], P(('groups', 'graph')), parts along dimension 0, may hold values from -6 to 6
- rotation: bfloat16 [235, 18432], P(None, ('groups', 'graph')), parts along dimension 1, may hold values from -1.75 to 1.75
- radial: bfloat16 [18432, 128], P(('groups', 'graph')), parts along dimension 0, may hold values from -6 to 6
- edge_source: int32 [18432], P(('groups', 'graph')), parts along dimension 0, may hold values from 0 to 79, as said below
- edge_valid: int32 [18432], P(('groups', 'graph')), parts along dimension 0, may hold values 0 or 1
- send_rows: int32 [128, 8], P(('groups', 'graph')), parts along dimension 0, may hold values from 0 to 47
- w_zero: bfloat16 [896, 896], replicated, may hold values from -0.1875 to 0.1875
- w_one: bfloat16 [768, 1536], replicated, may hold values from -0.15625 to 0.15625
- w_two: bfloat16 [640, 1280], replicated, may hold values from -0.15625 to 0.15625
Outputs:
- grad_nodes: bfloat16 [1536, 49, 128], P(('groups', 'graph')), parts along dimension 0
- grad_radial: bfloat16 [18432, 128], P(('groups', 'graph')), parts along dimension 0
- grad_w_zero: float32 [1605632], P(('groups', 'graph')), parts along dimension 0
- grad_w_one: float32 [2359296], P(('groups', 'graph')), parts along dimension 0
- grad_w_two: float32 [1638400], P(('groups', 'graph')), parts along dimension 0
There are 2 independent parts, one for each index of `groups`. A program takes and returns all parts, laid end to end along the dimension named above; an argument that names none is the same for every part. Nothing has to cross between parts.
Inputs may be any that keep to these rules, and one draw needn't show every extreme that they name: `edge_source`: A value v >= 48 names slot (v - 48) % 8 of the block that partition d - o_j sends to d, j = (v - 48) // 8; that partition exists.
All inputs are finite; a program needn't handle non-finite values. No bound on the sum of `edge_valid` on one device may be relied on, other than what follows from the above.
Results may differ from a plain program's by a relative error of at most 0.01.
Values may be sent and summed in bfloat16 or wider, within the bound.
A program may use at most 192 MiB of HBM per device.

v0:
```python
import functools

import jax
import jax.numpy as jnp
from jax import lax
from jax.experimental import pallas as pl
from jax.experimental.pallas import tpu as pltpu
from jax.sharding import PartitionSpec as P

BF = jnp.bfloat16
F32 = jnp.float32
peer_steps = (-2, -1, 1, 2)
order_first = (0, 6, 12, 17, 22)
CB = 32
VMEM_LIMIT = 58 * 2**20


def degrees():
    entry = 0
    for degree in range(7):
        held = min(2 * degree + 1, 5)
        yield degree, held, entry
        entry += held * (2 * degree + 1)


def shifted(block, distance):
    devices = range(lax.axis_size("graph"))
    route = [(i - distance, i) for i in devices if i - distance in devices]
    return lax.ppermute(block, "graph", route)


def dot(left, right):
    return jnp.dot(left, right, preferred_element_type=F32)


def dot_nt(left, right):
    return lax.dot_general(left, right, (((1,), (1,)), ((), ())), preferred_element_type=F32)


def dot_tn(left, right):
    return lax.dot_general(left, right, (((0,), (0,)), ((), ())), preferred_element_type=F32)


def rows(first, count):
    return pl.ds(pl.multiple_of(first, CB), count)


def forward_kernel(
    neigh, ch, widths,
    tab_ref, cot_ref, rot_ref, rad_ref, src_ref, valid_ref,
    gz_ref, g1_ref, g2_ref, rotated_ref, gout_ref,
    xg, cx, inp, rot32, radt,
):
    coefs, slots, _ = tab_ref.shape
    atoms = cot_ref.shape[1]
    ep = rot_ref.shape[1]
    hot = (lax.broadcasted_iota(jnp.int32, (slots, ep), 0) == src_ref[...]).astype(F32).astype(BF)
    edge = lax.broadcasted_iota(jnp.int32, (atoms, ep), 1)
    first = lax.broadcasted_iota(jnp.int32, (atoms, ep), 0) * neigh
    mine = (edge >= first) & (edge < first + neigh) & (valid_ref[...] != 0)
    rep = mine.astype(F32).astype(BF)
    rot32[...] = rot_ref[...].astype(F32)
    radt[...] = rad_ref[...].astype(F32).T

    def gather(n, _):
        at = pl.ds(pl.multiple_of(n * ch, ch), ch)
        xg[at, :] = dot_tn(tab_ref[n], hot).astype(BF)
        cx[at, :] = dot_tn(cot_ref[n], rep).astype(BF)
        return _

    lax.fori_loop(0, coefs, gather, 0)

    def rotate(step, _):
        eb = step // (ch // CB)
        cb = (step % (ch // CB)) * CB
        lanes = pl.ds(pl.multiple_of(eb * 128, 128), 128)
        rad = radt[rows(cb, CB), lanes]
        for degree, held, entry in degrees():
            acc = [None] * held
            accg = [None] * held
            for j in range(2 * degree + 1):
                at = rows((degree * degree + j) * ch + cb, CB)
                x = xg[at, lanes].astype(F32)
                g = cx[at, lanes].astype(F32)
                for m in range(held):
                    k = entry + m * (2 * degree + 1) + j
                    r = rot32[k : k + 1, lanes]
                    acc[m] = r * x if j == 0 else acc[m] + r * x
                    accg[m] = r * g if j == 0 else accg[m] + r * g
            for m in range(held):
                at = rows((order_first[m] + degree) * ch + cb, CB)
                rotated_ref[at, lanes] = acc[m].astype(BF)
                inp[at, lanes] = (acc[m] * rad).astype(BF)
                gout_ref[at, lanes] = accg[m].astype(BF)
        return _

    lax.fori_loop(0, (ep // 128) * (ch // CB), rotate, 0)

    wz, w1, w2 = widths
    half = wz // 2

    def zero_part(i, _):
        at = rows(i * half, half)
        gz_ref[at, :] = dot_nt(inp[at, :], gout_ref[0:wz, :]).astype(gz_ref.dtype)
        return _

    lax.fori_loop(0, 2, zero_part, 0)
    for width, base, out in ((w1, wz, g1_ref), (w2, wz + 2 * w1, g2_ref)):
        tile = width // 2
        plus = gout_ref.at[base : base + width]
        minus = gout_ref.at[base + width : base + 2 * width]

        def pair_part(i, _, width=width, base=base, out=out, tile=tile, plus=plus, minus=minus):
            p = inp[rows(base + i * tile, tile), :]
            m = inp[rows(base + width + i * tile, tile), :]
            at = rows(i * tile, tile)
            out[at, 0:width] = (dot_nt(p, plus[...]) + dot_nt(m, minus[...])).astype(out.dtype)
            out[at, width : 2 * width] = (dot_nt(p, minus[...]) - dot_nt(m, plus[...])).astype(out.dtype)
            return _

        lax.fori_loop(0, 2, pair_part, 0)


def backward_kernel(
    ch, widths,
    rot_ref, rad_ref, src_ref, gout_ref, rotated_ref, w0_ref, w1_ref, w2_ref,
    sum_ref, grad_ref,
    gin, eg, rot32, radt, grt,
):
    coefs, slots, _ = sum_ref.shape
    ep = rot_ref.shape[1]
    edges = grad_ref.shape[0]
    hot = (lax.broadcasted_iota(jnp.int32, (slots, ep), 0) == src_ref[...]).astype(F32).astype(BF)
    rot32[...] = rot_ref[...].astype(F32)
    radt[...] = rad_ref[...].astype(F32).T
    wz, w1, w2 = widths
    half = wz // 2

    def zero_part(i, _):
        at = rows(i * half, half)
        gin[at, :] = dot(w0_ref[at, :], gout_ref[0:wz, :])
        return _

    lax.fori_loop(0, 2, zero_part, 0)
    for width, base, w_ref in ((w1, wz, w1_ref), (w2, wz + 2 * w1, w2_ref)):
        tile = width // 2
        plus = gout_ref.at[base : base + width]
        minus = gout_ref.at[base + width : base + 2 * width]

        def pair_part(i, _, width=width, base=base, w_ref=w_ref, tile=tile, plus=plus, minus=minus):
            at = rows(i * tile, tile)
            a = w_ref[at, 0:width]
            b = w_ref[at, width : 2 * width]
            gin[rows(base + i * tile, tile), :] = dot(a, plus[...]) + dot(b, minus[...])
            gin[rows(base + width + i * tile, tile), :] = dot(a, minus[...]) - dot(b, plus[...])
            return _

        lax.fori_loop(0, 2, pair_part, 0)

    def rotate(step, _):
        eb = step // (ch // CB)
        cb = (step % (ch // CB)) * CB
        lanes = pl.ds(pl.multiple_of(eb * 128, 128), 128)
        rad = radt[rows(cb, CB), lanes]
        total = jnp.zeros((CB, 128), F32)
        for degree, held, entry in degrees():
            weighted = []
            for m in range(held):
                at = rows((order_first[m] + degree) * ch + cb, CB)
                value = gin[at, lanes]
                total = total + value * rotated_ref[at, lanes].astype(F32)
                weighted.append(value * rad)
            for j in range(2 * degree + 1):
                acc = None
                for m in range(held):
                    k = entry + m * (2 * degree + 1) + j
                    term = rot32[k : k + 1, lanes] * weighted[m]
                    acc = term if m == 0 else acc + term
                eg[rows((degree * degree + j) * ch + cb, CB), lanes] = acc.astype(BF)
        grt[rows(cb, CB), lanes] = total
        return _

    lax.fori_loop(0, (ep // 128) * (ch // CB), rotate, 0)
    grad_ref[...] = grt[...].T[:edges].astype(BF)

    def scatter(i, _):
        part = dot_nt(hot, eg[pl.ds(pl.multiple_of(i * 7 * ch, ch), 7 * ch), :])
        for j in range(7):
            sum_ref[i * 7 + j] = part[:, j * ch : (j + 1) * ch]
        return _

    lax.fori_loop(0, coefs // 7, scatter, 0)


def body(node_irreps, cotangent, rotation, radial, edge_source, edge_valid, send_rows, w_zero, w_one, w_two):
    atoms, coefs, ch = node_irreps.shape
    halo = send_rows.shape[1]
    edges = edge_source.shape[0]
    neigh = edges // atoms
    ep = -(-edges // 128) * 128
    pad = ep - edges
    slots = atoms + 4 * halo
    widths = (w_zero.shape[0], w_one.shape[0], w_two.shape[0])
    feats = widths[0] + 2 * widths[1] + 2 * widths[2]
    send_hot = (send_rows.reshape(-1)[:, None] == jnp.arange(atoms, dtype=jnp.int32)[None, :]).astype(BF)
    nodes = node_irreps.transpose(1, 0, 2)
    cots = cotangent.transpose(1, 0, 2)
    outgoing = jnp.einsum("sa,nac->nsc", send_hot, nodes, preferred_element_type=F32).astype(BF)
    incoming = [shifted(outgoing[:, i * halo : (i + 1) * halo], peer_steps[i]) for i in range(4)]
    table = jnp.concatenate([nodes, *incoming], axis=1)
    rot = jnp.pad(rotation, ((0, 0), (0, pad)))
    rad = jnp.pad(radial, ((0, pad), (0, 0)))
    src = jnp.pad(edge_source, (0, pad), constant_values=-1)[None, :]
    valid = jnp.pad(edge_valid, (0, pad))[None, :]
    packed = rotation.shape[0]
    params = pltpu.CompilerParams(vmem_limit_bytes=VMEM_LIMIT)
    whole = pl.BlockSpec(memory_space=pltpu.VMEM)
    gz, g1, g2, rotated, gout = pl.pallas_call(
        functools.partial(forward_kernel, neigh, ch, widths),
        out_shape=(
            jax.ShapeDtypeStruct(w_zero.shape, BF),
            jax.ShapeDtypeStruct(w_one.shape, BF),
            jax.ShapeDtypeStruct(w_two.shape, BF),
            jax.ShapeDtypeStruct((feats, ep), BF),
            jax.ShapeDtypeStruct((feats, ep), BF),
        ),
        in_specs=[whole] * 6,
        out_specs=[whole] * 5,
        scratch_shapes=[
            pltpu.VMEM((coefs * ch, ep), BF),
            pltpu.VMEM((coefs * ch, ep), BF),
            pltpu.VMEM((feats, ep), BF),
            pltpu.VMEM((packed, ep), F32),
            pltpu.VMEM((ch, ep), F32),
        ],
        compiler_params=params,
        name="forward",
    )(table, cots, rot, rad, src, valid)
    grads = [
        lax.psum_scatter(g.reshape(-1), "graph", scatter_dimension=0, tiled=True).astype(F32)
        for g in (gz, g1, g2)
    ]
    summed, grad_radial = pl.pallas_call(
        functools.partial(backward_kernel, ch, widths),
        out_shape=(
            jax.ShapeDtypeStruct((coefs, slots, ch), F32),
            jax.ShapeDtypeStruct((edges, ch), BF),
        ),
        in_specs=[whole] * 8,
        out_specs=[whole] * 2,
        scratch_shapes=[
            pltpu.VMEM((feats, ep), F32),
            pltpu.VMEM((coefs * ch, ep), BF),
            pltpu.VMEM((packed, ep), F32),
            pltpu.VMEM((ch, ep), F32),
            pltpu.VMEM((ch, ep), F32),
        ],
        compiler_params=params,
        cost_estimate=pl.CostEstimate(flops=8_000_000_000, bytes_accessed=20_000_000, transcendentals=0),
        name="backward",
    )(rot, rad, src, gout, rotated, w_zero, w_one, w_two)
    slot_grad = summed[:, atoms:].astype(BF)
    returned = jnp.concatenate(
        [shifted(slot_grad[:, i * halo : (i + 1) * halo], -peer_steps[i]) for i in range(4)], axis=1
    )
    added = jnp.einsum("sa,nsc->nac", send_hot, returned, preferred_element_type=F32)
    total = cots.astype(F32) + summed[:, :atoms] + added
    grad_nodes = total.astype(BF).transpose(1, 0, 2)
    return (grad_nodes, grad_radial, *grads)


def solution(mesh):
    both = ("groups", "graph")
    return jax.shard_map(
        body,
        mesh=mesh,
        in_specs=(
            P(both, None, None), P(both, None, None), P(None, both), P(both, None),
            P(both), P(both), P(both, None), P(), P(), P(),
        ),
        out_specs=(P(both, None, None), P(both, None), P(both), P(both), P(both)),
        check_vma=False,
    )
```

profile of v0, /device:TPU:8, one launch (start us, length us, event | category | flops | bytes accessed | tf_op | source)
XLA Modules:
  0.0 224.9 jit_solution(12868833595988332003)
XLA Ops:
  7.2 0.8 eq.15
  8.1 1.4 fusion.3
  9.6 3.3 %collective-permute-start = (bf16[49,8,128]{2,1,0:T(8,128)(2,1)S(1)}, bf16[49,8,128]{2,1,0:T(8,128)(2,1)S(1)}, u32[]{:S(2)}, u32[]{:S(2)}) collective-permute-start(bf16[49,8,128]{2,1,0:T(8,128)(2,1)S(1)} %get-tuple-element.29), channel_id=1, source_target_pairs={{2,0},{3,1},{4,2},{5,3},{6,4},{7,5},{8,6},{9,7},{10,8},{11,9},{12,... | collective-permute-start | bytes 301064 | tf_op jit(solution)/shard_map/ppermute | solution.py:29
  12.9 1.9 collective-permute-start.1
  14.8 2.4 %collective-permute-start.2 = (bf16[49,8,128]{2,1,0:T(8,128)(2,1)S(1)}, bf16[49,8,128]{2,1,0:T(8,128)(2,1)S(1)}, u32[]{:S(2)}, u32[]{:S(2)}) collective-permute-start(bf16[49,8,128]{2,1,0:T(8,128)(2,1)S(1)} %get-tuple-element.27), channel_id=1, source_target_pairs={{0,1},{1,2},{2,3},{3,4},{4,5},{5,6},{6,7},{7,8},{8,9},{9,10},{10,1... | collective-permute-start | bytes 301064 | tf_op jit(solution)/shard_map/ppermute | solution.py:29
  17.2 2.6 %collective-permute-start.3 = (bf16[49,8,128]{2,1,0:T(8,128)(2,1)S(1)}, bf16[49,8,128]{2,1,0:T(8,128)(2,1)S(1)}, u32[]{:S(2)}, u32[]{:S(2)}) collective-permute-start(bf16[49,8,128]{2,1,0:T(8,128)(2,1)S(1)} %get-tuple-element.26), channel_id=1, source_target_pairs={{0,2},{1,3},{2,4},{3,5},{4,6},{5,7},{6,8},{7,9},{8,10},{9,11},{10,... | collective-permute-start | bytes 301064 | tf_op jit(solution)/shard_map/ppermute | solution.py:29
  20.1 0.8 pad.15.rot_ref
  22.8 2.7 %collective-permute-done.3 = bf16[49,8,128]{2,1,0:T(8,128)(2,1)S(1)} collective-permute-done((bf16[49,8,128]{2,1,0:T(8,128)(2,1)S(1)}, bf16[49,8,128]{2,1,0:T(8,128)(2,1)S(1)}, u32[]{:S(2)}, u32[]{:S(2)}) %collective-permute-start.3) | collective-permute-done | bytes 100384 | tf_op jit(solution)/shard_map/ppermute | solution.py:29
  25.6 1.0 copy-done.1
  26.6 41.1 %forward.1 = (bf16[896,896]{1,0:T(8,128)(2,1)}, bf16[768,1536]{1,0:T(8,128)(2,1)}, bf16[640,1280]{1,0:T(8,128)(2,1)}, bf16[3712,640]{1,0:T(8,128)(2,1)}, bf16[3712,640]{1,0:T(8,128)(2,1)}) custom-call(bf16[49,80,128]{2,1,0:T(8,128)(2,1)} %copy-done.1, bf16[49,48,128]{2,1,0:T(8,128)(2,1)} %bitcast.23, bf16[235,640]{1,0:T(8,128)(2,1)} %pad.15.rot_ref, ...), custom_call_target="tpu_custom_call" | custom-call | tf_op jit(solution)/shard_map/forward/pallas_call | solution.py:218
  67.7 5.7 %reshape.21 = bf16[1179648]{0:T(1024)(128)(2,1)} reshape(bf16[768,1536]{1,0:T(8,128)(2,1)} %get-tuple-element.17) | data formatting | bytes 4718592 | tf_op jit(solution)/shard_map/reshape | solution.py:240
  73.4 3.1 %reshape.22 = bf16[819200]{0:T(1024)(128)(2,1)} reshape(bf16[640,1280]{1,0:T(8,128)(2,1)S(1)} %copy-done.4) | data formatting | bytes 3276800 | tf_op jit(solution)/shard_map/reshape | solution.py:240
  76.5 2.7 %reshape.20 = bf16[802816]{0:T(1024)(128)(2,1)} reshape(bf16[896,896]{1,0:T(8,128)(2,1)S(1)} %copy-done.5) | data formatting | bytes 3211264 | tf_op jit(solution)/shard_map/reshape | solution.py:240
  79.2 26.7 %backward.1 = (f32[49,80,128]{2,1,0:T(8,128)}, bf16[576,128]{1,0:T(8,128)(2,1)}) custom-call(bf16[235,640]{1,0:T(8,128)(2,1)} %pad.15.rot_ref, bf16[640,128]{1,0:T(8,128)(2,1)} %pad.16.rad_ref, s32[1,640]{1,0:T(1,128)} %broadcast_in_dim.7.src_ref, bf16[3712,640]{1,0:T(8,128)(2,1)} %get-tuple-element.12.gout_ref, ...), custom_call_target="tpu_custom_call" | custom-call | flops 8000000000 | bytes 20000000 | tf_op jit(solution)/shard_map/backward/pallas_call | solution.py:243
  106.0 1.9 convert.3
  107.9 1.9 collective-permute-start.4
  109.8 1.9 collective-permute-start.5
  111.8 4.5 %collective-permute-start.6 = (bf16[49,8,128]{2,1,0:T(8,128)(2,1)S(1)}, bf16[49,8,128]{2,1,0:T(8,128)(2,1)S(1)}, u32[]{:S(2)}, u32[]{:S(2)}) collective-permute-start(bf16[49,8,128]{2,1,0:T(8,128)(2,1)S(1)} %get-tuple-element.24), channel_id=1, source_target_pairs={{1,0},{2,1},{3,2},{4,3},{5,4},{6,5},{7,6},{8,7},{9,8},{10,9},{11,1... | collective-permute-start | bytes 301064 | tf_op jit(solution)/shard_map/ppermute | solution.py:29
  116.3 3.9 %collective-permute-start.7 = (bf16[49,8,128]{2,1,0:T(8,128)(2,1)S(1)}, bf16[49,8,128]{2,1,0:T(8,128)(2,1)S(1)}, u32[]{:S(2)}, u32[]{:S(2)}) collective-permute-start(bf16[49,8,128]{2,1,0:T(8,128)(2,1)S(1)} %get-tuple-element.23), channel_id=1, source_target_pairs={{2,0},{3,1},{4,2},{5,3},{6,4},{7,5},{8,6},{9,7},{10,8},{11,9},{12,... | collective-permute-start | bytes 301064 | tf_op jit(solution)/shard_map/ppermute | solution.py:29
  123.5 1.3 fusion.2
  124.8 88.4 %all-reduce.10.cloned.1.call-done = (bf16[802816]{0:T(1024)(128)(2,1)}, bf16[1179648]{0:T(1024)(128)(2,1)}, bf16[819200]{0:T(1024)(128)(2,1)}) async-done(((bf16[802816]{0:T(1024)(128)(2,1)}, bf16[1179648]{0:T(1024)(128)(2,1)}, bf16[819200]{0:T(1024)(128)(2,1)}), (bf16[802816]{0:T(1024)(128)(2,1)}, bf16[1179648]{0:T(1024)(128)(2,1)}, bf16[819200]{0:T(1024)(128)(2,1)})) %all-reduce.10.cloned.1.call-update) | async-done | bytes 5603344
  213.2 1.6 dynamic-slice_convert_fusion
  214.8 1.6 dynamic-slice_convert_fusion.1
  216.4 1.6 dynamic-slice_convert_fusion.2
  (44 shorter events, 3.8 us)
Async XLA Ops:
  7.2 12.7 %copy-start.2 = (bf16[48,49,128]{2,0,1:T(8,128)(2,1)S(1)}, bf16[48,49,128]{2,0,1:T(8,128)(2,1)}, u32[]{:S(2)}) copy-start(bf16[48,49,128]{2,0,1:T(8,128)(2,1)} %param.10) | copy-start | bytes 1806340
  7.2 12.7 %copy-start.6 = (bf16[235,576]{0,1:T(8,128)(2,1)S(1)}, bf16[235,576]{0,1:T(8,128)(2,1)}, u32[]{:S(2)}) copy-start(bf16[235,576]{0,1:T(8,128)(2,1)} %param.12) | copy-start | bytes 812164
  7.2 206.0 %all-reduce.10.cloned.1.call-start = ((), (), s32[]{:S(2)}) async-start(), calls=%async_computation | async-start | bytes 11206656
  9.5 11.4 %copy-start.7 = (bf16[576,128]{1,0:T(8,128)(2,1)S(1)}, bf16[576,128]{1,0:T(8,128)(2,1)}, u32[]{:S(2)}) copy-start(bf16[576,128]{1,0:T(8,128)(2,1)} %param.13) | copy-start | bytes 442372
  9.5 12.1 %copy-start.8 = (s32[576]{0:T(1024)S(1)}, s32[576]{0:T(1024)}, u32[]{:S(2)}) copy-start(s32[576]{0:T(1024)} %param.14) | copy-start | bytes 6916
  9.5 12.7 %copy-start.9 = (s32[576]{0:T(1024)S(1)}, s32[576]{0:T(1024)}, u32[]{:S(2)}) copy-start(s32[576]{0:T(1024)} %param.15) | copy-start | bytes 6916
  9.6 13.2 %collective-permute-start = (bf16[49,8,128]{2,1,0:T(8,128)(2,1)S(1)}, bf16[49,8,128]{2,1,0:T(8,128)(2,1)S(1)}, u32[]{:S(2)}, u32[]{:S(2)}) collective-permute-start(bf16[49,8,128]{2,1,0:T(8,128)(2,1)S(1)} %get-tuple-element.29), channel_id=1, source_target_pairs={{2,0},{3,1},{4,2},{5,3},{6,4},{7,5},{8,6},{9,7},{10,8},{11,9},{12,... | collective-permute-start | bytes 301064 | tf_op jit(solution)/shard_map/ppermute | solution.py:29
  12.9 9.9 %collective-permute-start.1 = (bf16[49,8,128]{2,1,0:T(8,128)(2,1)S(1)}, bf16[49,8,128]{2,1,0:T(8,128)(2,1)S(1)}, u32[]{:S(2)}, u32[]{:S(2)}) collective-permute-start(bf16[49,8,128]{2,1,0:T(8,128)(2,1)S(1)} %get-tuple-element.28), channel_id=1, source_target_pairs={{1,0},{2,1},{3,2},{4,3},{5,4},{6,5},{7,6},{8,7},{9,8},{10,9},{11,1... | collective-permute-start | bytes 301064 | tf_op jit(solution)/shard_map/ppermute | solution.py:29
  14.8 8.0 %collective-permute-start.2 = (bf16[49,8,128]{2,1,0:T(8,128)(2,1)S(1)}, bf16[49,8,128]{2,1,0:T(8,128)(2,1)S(1)}, u32[]{:S(2)}, u32[]{:S(2)}) collective-permute-start(bf16[49,8,128]{2,1,0:T(8,128)(2,1)S(1)} %get-tuple-element.27), channel_id=1, source_target_pairs={{0,1},{1,2},{2,3},{3,4},{4,5},{5,6},{6,7},{7,8},{8,9},{9,10},{10,1... | collective-permute-start | bytes 301064 | tf_op jit(solution)/shard_map/ppermute | solution.py:29
  17.2 8.3 %collective-permute-start.3 = (bf16[49,8,128]{2,1,0:T(8,128)(2,1)S(1)}, bf16[49,8,128]{2,1,0:T(8,128)(2,1)S(1)}, u32[]{:S(2)}, u32[]{:S(2)}) collective-permute-start(bf16[49,8,128]{2,1,0:T(8,128)(2,1)S(1)} %get-tuple-element.26), channel_id=1, source_target_pairs={{0,2},{1,3},{2,4},{3,5},{4,6},{5,7},{6,8},{7,9},{8,10},{9,11},{10,... | collective-permute-start | bytes 301064 | tf_op jit(solution)/shard_map/ppermute | solution.py:29
  25.6 1.0 copy-start.1
  67.7 5.7 %copy-start.4 = (bf16[640,1280]{1,0:T(8,128)(2,1)S(1)}, bf16[640,1280]{1,0:T(8,128)(2,1)}, u32[]{:S(2)}) copy-start(bf16[640,1280]{1,0:T(8,128)(2,1)} %get-tuple-element.18) | copy-start | bytes 4915204
  73.4 3.1 %copy-start.5 = (bf16[896,896]{1,0:T(8,128)(2,1)S(1)}, bf16[896,896]{1,0:T(8,128)(2,1)}, u32[]{:S(2)}) copy-start(bf16[896,896]{1,0:T(8,128)(2,1)} %get-tuple-element.16) | copy-start | bytes 4816900
  106.0 14.3 %copy-start.10 = (u32[32]{0:T(128)S(1)}, u32[32]{0:T(128)}, u32[]{:S(2)}) copy-start(u32[32]{0:T(128)} %constant.19) | copy-start | bytes 388
  106.0 17.6 %copy-start = (f32[49,80,128]{2,1,0:T(8,128)S(1)}, f32[49,80,128]{2,1,0:T(8,128)}, u32[]{:S(2)}) copy-start(f32[49,80,128]{2,1,0:T(8,128)} %get-tuple-element.14) | copy-start | bytes 6021124
  106.0 17.6 %copy-start.3 = (bf16[48,49,128]{2,0,1:T(8,128)(2,1)S(1)}, bf16[48,49,128]{2,0,1:T(8,128)(2,1)}, u32[]{:S(2)}) copy-start(bf16[48,49,128]{2,0,1:T(8,128)(2,1)} %param.11) | copy-start | bytes 1806340
  107.9 14.9 %collective-permute-start.4 = (bf16[49,8,128]{2,1,0:T(8,128)(2,1)S(1)}, bf16[49,8,128]{2,1,0:T(8,128)(2,1)S(1)}, u32[]{:S(2)}, u32[]{:S(2)}) collective-permute-start(bf16[49,8,128]{2,1,0:T(8,128)(2,1)S(1)} %get-tuple-element.22), channel_id=1, source_target_pairs={{0,2},{1,3},{2,4},{3,5},{4,6},{5,7},{6,8},{7,9},{8,10},{9,11},{10,... | collective-permute-start | bytes 301064 | tf_op jit(solution)/shard_map/ppermute | solution.py:29
  109.8 13.0 %collective-permute-start.5 = (bf16[49,8,128]{2,1,0:T(8,128)(2,1)S(1)}, bf16[49,8,128]{2,1,0:T(8,128)(2,1)S(1)}, u32[]{:S(2)}, u32[]{:S(2)}) collective-permute-start(bf16[49,8,128]{2,1,0:T(8,128)(2,1)S(1)} %get-tuple-element.25), channel_id=1, source_target_pairs={{0,1},{1,2},{2,3},{3,4},{4,5},{5,6},{6,7},{7,8},{8,9},{9,10},{10,1... | collective-permute-start | bytes 301064 | tf_op jit(solution)/shard_map/ppermute | solution.py:29
  111.8 11.0 %collective-permute-start.6 = (bf16[49,8,128]{2,1,0:T(8,128)(2,1)S(1)}, bf16[49,8,128]{2,1,0:T(8,128)(2,1)S(1)}, u32[]{:S(2)}, u32[]{:S(2)}) collective-permute-start(bf16[49,8,128]{2,1,0:T(8,128)(2,1)S(1)} %get-tuple-element.24), channel_id=1, source_target_pairs={{1,0},{2,1},{3,2},{4,3},{5,4},{6,5},{7,6},{8,7},{9,8},{10,9},{11,1... | collective-permute-start | bytes 301064 | tf_op jit(solution)/shard_map/ppermute | solution.py:29
  116.3 7.2 %collective-permute-start.7 = (bf16[49,8,128]{2,1,0:T(8,128)(2,1)S(1)}, bf16[49,8,128]{2,1,0:T(8,128)(2,1)S(1)}, u32[]{:S(2)}, u32[]{:S(2)}) collective-permute-start(bf16[49,8,128]{2,1,0:T(8,128)(2,1)S(1)} %get-tuple-element.23), channel_id=1, source_target_pairs={{2,0},{3,1},{4,2},{5,3},{6,4},{7,5},{8,6},{9,7},{10,8},{11,9},{12,... | collective-permute-start | bytes 301064 | tf_op jit(solution)/shard_map/ppermute | solution.py:29
Sparse Core Ops, SparseCore 0:
  79.4 133.7 all-reduce.9
where the time goes:
time: 227 us; the launch traced here: 225 us
  waiting for transfers between devices  91.9 us (40%)
  Pallas kernels  67.8 us (30%)
  starting transfers between devices  22.6 us (10%)
  local copies, waits for them, and re-layouts  17.1 us (8%)
  between operations  16.2 us (7%)
  other arithmetic  6.67 us (3%)
  matrix products  2.64 us (1%)
    unnamed x2, waiting for transfers between devices  88.4 us
    pallas_call x1, Pallas kernels, body(): pl.pallas_call(functools.partial(forward_kernel, neigh, ch, widths), out_...  41.1 us
    pallas_call x1, Pallas kernels, body(): pl.pallas_call(functools.partial(backward_kernel, ch, widths), out_shape=...  26.7 us
    ppermute x8, starting transfers between devices, shifted(): return lax.ppermute(block, 'graph', route)  22.5 us
    reshape x3, local copies, waits for them, and re-layouts, body(): g.reshape(-1)  11.5 us
    convert_element_type x3, other arithmetic, body(): lax.psum_scatter(g.reshape(-1), 'graph', scatter_dimension=0, tiled=True)  4.82 us
  transfers between devices with their start and end apart: 9, of which 3 were waited for; matrix products, arithmetic and copies ran while one was open for 3% of the time, Pallas kernels for 12%

commit v1 on v0

--- a/solution.py
+++ b/solution.py
@@ -192,27 +192,263 @@
     lax.fori_loop(0, coefs // 7, scatter, 0)
 
 
-def body(node_irreps, cotangent, rotation, radial, edge_source, edge_valid, send_rows, w_zero, w_one, w_two):
-    atoms, coefs, ch = node_irreps.shape
-    halo = send_rows.shape[1]
-    edges = edge_source.shape[0]
-    neigh = edges // atoms
-    ep = -(-edges // 128) * 128
-    pad = ep - edges
-    slots = atoms + 4 * halo
-    widths = (w_zero.shape[0], w_one.shape[0], w_two.shape[0])
+def fused_kernel(
+    neigh, ch, widths, graph,
+    tab_ref, cot_ref, rot_ref, rad_ref, src_ref, valid_ref, w0_ref, w1_ref, w2_ref,
+    sum_ref, grad_ref, oz_ref, o1_ref, o2_ref,
+    xg, cx, inp, gout, rotated, rot32, radt, grt, *rest,
+):
+    staged = rest[0:3]
+    landed = (rest[3:7], rest[7:11], rest[11:15])
+    send_sem, recv_sem = rest[15], rest[16]
+    outs = (oz_ref, o1_ref, o2_ref)
+    me = lax.axis_index("graph")
+    bits = [me & 1, (me >> 1) & 1, (me >> 2) & 1, (me >> 3) & 1]
+    partners = [me + (1 << b) * (1 - 2 * bits[b]) for b in range(4)]
+    barrier = pltpu.get_barrier_semaphore()
+    for partner in partners:
+        pl.semaphore_signal(barrier, inc=1, device_id={"graph": partner}, device_id_type=pl.DeviceIdType.MESH)
+
+    firsts = [0]
+    for stage in range(4):
+        firsts.append(firsts[-1] + bits[stage] * (8 >> stage))
+
+    def copy_of(which, stage):
+        count = 8 >> stage
+        at = firsts[stage] + (1 - bits[stage]) * count
+        return pltpu.make_async_remote_copy(
+            src_ref=staged[which].at[pl.ds(at, count)],
+            dst_ref=landed[which][stage],
+            send_sem=send_sem.at[which * 4 + stage],
+            recv_sem=recv_sem.at[which * 4 + stage],
+            device_id={"graph": partners[stage]},
+            device_id_type=pl.DeviceIdType.MESH,
+        )
+
+    def advance(which, stage):
+        copy_of(which, stage).wait_recv()
+        count = 8 >> stage
+        if stage == 3:
+            outs[which][...] = staged[which][firsts[4]].astype(F32) + landed[which][3][0].astype(F32)
+            return
+        buffer, part, first = staged[which], landed[which][stage], firsts[stage + 1]
+
+        def add(i, _):
+            buffer[first + i] = (buffer[first + i].astype(F32) + part[i].astype(F32)).astype(BF)
+            return _
+
+        lax.fori_loop(0, count, add, 0)
+        copy_of(which, stage + 1).start()
+
+    coefs, slots, _ = tab_ref.shape
+    atoms = cot_ref.shape[1]
+    ep = rot_ref.shape[1]
+    edges = grad_ref.shape[0]
+    wz, w1, w2 = widths
+    hot = (lax.broadcasted_iota(jnp.int32, (slots, ep), 0) == src_ref[...]).astype(F32).astype(BF)
+    edge = lax.broadcasted_iota(jnp.int32, (atoms, ep), 1)
+    first_edge = lax.broadcasted_iota(jnp.int32, (atoms, ep), 0) * neigh
+    mine = (edge >= first_edge) & (edge < first_edge + neigh) & (valid_ref[...] != 0)
+    rep = mine.astype(F32).astype(BF)
+    rot32[...] = rot_ref[...].astype(F32)
+    radt[...] = rad_ref[...].astype(F32).T
+
+    def gather(n, _):
+        at = pl.ds(pl.multiple_of(n * ch, ch), ch)
+        xg[at, :] = dot_tn(tab_ref[n], hot).astype(BF)
+        cx[at, :] = dot_tn(cot_ref[n], rep).astype(BF)
+        return _
+
+    lax.fori_loop(0, coefs, gather, 0)
+
+    def rotate(step, _):
+        eb = step // (ch // CB)
+        cb = (step % (ch // CB)) * CB
+        lanes = pl.ds(pl.multiple_of(eb * 128, 128), 128)
+        rad = radt[rows(cb, CB), lanes]
+        for degree, held, entry in degrees():
+            acc = [None] * held
+            accg = [None] * held
+            for j in range(2 * degree + 1):
+                at = rows((degree * degree + j) * ch + cb, CB)
+                x = xg[at, lanes].astype(F32)
+                g = cx[at, lanes].astype(F32)
+                for m in range(held):
+                    k = entry + m * (2 * degree + 1) + j
+                    r = rot32[k : k + 1, lanes]
+                    acc[m] = r * x if j == 0 else acc[m] + r * x
+                    accg[m] = r * g if j == 0 else accg[m] + r * g
+            for m in range(held):
+                at = rows((order_first[m] + degree) * ch + cb, CB)
+                rotated[at, lanes] = acc[m].astype(BF)
+                inp[at, lanes] = (acc[m] * rad).astype(BF)
+                gout[at, lanes] = accg[m].astype(BF)
+        return _
+
+    lax.fori_loop(0, (ep // 128) * (ch // CB), rotate, 0)
+
+    def place(which, i, columns, value):
+        height = value.shape[0] // 8
+        for jj in range(8):
+            position = (jj & 1) * 8 + ((jj >> 1) & 1) * 4 + ((jj >> 2) & 1) * 2 + i
+            staged[which][position, :, columns] = value[jj * height : (jj + 1) * height].astype(BF)
+
+    def weight_zero():
+        half = wz // 2
+
+        def part(i, _):
+            place(0, i, slice(0, wz), dot_nt(inp[rows(i * half, half), :], gout[0:wz, :]))
+            return _
+
+        lax.fori_loop(0, 2, part, 0)
+
+    def weight_pair(which, width, base):
+        tile = width // 2
+        plus = gout.at[base : base + width]
+        minus = gout.at[base + width : base + 2 * width]
+
+        def part(i, _):
+            p = inp[rows(base + i * tile, tile), :]
+            m = inp[rows(base + width + i * tile, tile), :]
+            place(which, i, slice(0, width), dot_nt(p, plus[...]) + dot_nt(m, minus[...]))
+            place(which, i, slice(width, 2 * width), dot_nt(p, minus[...]) - dot_nt(m, plus[...]))
+            return _
+
+        lax.fori_loop(0, 2, part, 0)
+
+    gin = cx
+
+    def back_zero():
+        half = wz // 2
+
+        def part(i, _):
+            at = rows(i * half, half)
+            gin[at, :] = dot(w0_ref[at, :], gout[0:wz, :]).astype(BF)
+            return _
+
+        lax.fori_loop(0, 2, part, 0)
+
+    def back_pair(width, base, w_ref):
+        tile = width // 2
+        plus = gout.at[base : base + width]
+        minus = gout.at[base + width : base + 2 * width]
+
+        def part(i, _):
+            at = rows(i * tile, tile)
+            a = w_ref[at, 0:width]
+            b = w_ref[at, width : 2 * width]
+            gin[rows(base + i * tile, tile), :] = (dot(a, plus[...]) + dot(b, minus[...])).astype(BF)
+            gin[rows(base + width + i * tile, tile), :] = (dot(a, minus[...]) - dot(b, plus[...])).astype(BF)
+            return _
+
+        lax.fori_loop(0, 2, part, 0)
+
+    weight_pair(1, w1, wz)
+    pl.semaphore_wait(barrier, 4)
+    copy_of(1, 0).start()
+    weight_pair(2, w2, wz + 2 * w1)
+    copy_of(2, 0).start()
+    advance(1, 0)
+    weight_zero()
+    copy_of(0, 0).start()
+    advance(2, 0)
+    back_zero()
+    advance(0, 0)
+    back_pair(w1, wz, w1_ref)
+    advance(1, 1)
+    back_pair(w2, wz + 2 * w1, w2_ref)
+
+    eg = xg
+
+    def rotate_back(step, _):
+        eb = step // (ch // CB)
+        cb = (step % (ch // CB)) * CB
+        lanes = pl.ds(pl.multiple_of(eb * 128, 128), 128)
+        rad = radt[rows(cb, CB), lanes]
+        total = jnp.zeros((CB, 128), F32)
+        for degree, held, entry in degrees():
+            weighted = []
+            for m in range(held):
+                at = rows((order_first[m] + degree) * ch + cb, CB)
+                value = gin[at, lanes].astype(F32)
+                total = total + value * rotated[at, lanes].astype(F32)
+                weighted.append(value * rad)
+            for j in range(2 * degree + 1):
+                acc = None
+                for m in range(held):
+                    k = entry + m * (2 * degree + 1) + j
+                    term = rot32[k : k + 1, lanes] * weighted[m]
+                    acc = term if m == 0 else acc + term
+                eg[rows((degree * degree + j) * ch + cb, CB), lanes] = acc.astype(BF)
+        grt[rows(cb, CB), lanes] = total
+        return _
+
+    steps = (ep // 128) * (ch // CB)
+    lax.fori_loop(0, steps // 2, rotate_back, 0)
+    advance(2, 1)
+    advance(1, 2)
+    lax.fori_loop(steps // 2, steps, rotate_back, 0)
+    advance(0, 1)
+    advance(2, 2)
+    grad_ref[...] = grt[...].T[:edges].astype(BF)
+
+    def scatter(i, _):
+        part = dot_nt(hot, eg[pl.ds(pl.multiple_of(i * 7 * ch, ch), 7 * ch), :])
+        for j in range(7):
+            sum_ref[i * 7 + j] = part[:, j * ch : (j + 1) * ch]
+        return _
+
+    lax.fori_loop(0, coefs // 7, scatter, 0)
+    advance(1, 3)
+    advance(0, 2)
+    advance(2, 3)
+    advance(0, 3)
+    for which in range(3):
+        for stage in range(4):
+            copy_of(which, stage).wait_send()
+
+
+def fused(neigh, ch, widths, graph, table, cots, rot, rad, src, valid, weights, edges):
+    coefs, slots, _ = table.shape
+    packed, ep = rot.shape
     feats = widths[0] + 2 * widths[1] + 2 * widths[2]
-    send_hot = (send_rows.reshape(-1)[:, None] == jnp.arange(atoms, dtype=jnp.int32)[None, :]).astype(BF)
-    nodes = node_irreps.transpose(1, 0, 2)
-    cots = cotangent.transpose(1, 0, 2)
-    outgoing = jnp.einsum("sa,nac->nsc", send_hot, nodes, preferred_element_type=F32).astype(BF)
-    incoming = [shifted(outgoing[:, i * halo : (i + 1) * halo], peer_steps[i]) for i in range(4)]
-    table = jnp.concatenate([nodes, *incoming], axis=1)
-    rot = jnp.pad(rotation, ((0, 0), (0, pad)))
-    rad = jnp.pad(radial, ((0, pad), (0, 0)))
-    src = jnp.pad(edge_source, (0, pad), constant_values=-1)[None, :]
-    valid = jnp.pad(edge_valid, (0, pad))[None, :]
-    packed = rotation.shape[0]
+    whole = pl.BlockSpec(memory_space=pltpu.VMEM)
+    parts = [(w.shape[0] // graph, w.shape[1]) for w in weights]
+    scratch = [
+        pltpu.VMEM((coefs * ch, ep), BF),
+        pltpu.VMEM((coefs * ch, ep), BF),
+        pltpu.VMEM((feats, ep), BF),
+        pltpu.VMEM((feats, ep), BF),
+        pltpu.VMEM((feats, ep), BF),
+        pltpu.VMEM((packed, ep), F32),
+        pltpu.VMEM((ch, ep), F32),
+        pltpu.VMEM((ch, ep), F32),
+    ]
+    scratch += [pltpu.VMEM((graph, *part), BF) for part in parts]
+    scratch += [pltpu.VMEM((8 >> stage, *part), BF) for part in parts for stage in range(4)]
+    scratch += [pltpu.SemaphoreType.DMA((12,)), pltpu.SemaphoreType.DMA((12,))]
+    return pl.pallas_call(
+        functools.partial(fused_kernel, neigh, ch, widths, graph),
+        out_shape=(
+            jax.ShapeDtypeStruct((coefs, slots, ch), F32),
+            jax.ShapeDtypeStruct((edges, ch), BF),
+            *(jax.ShapeDtypeStruct(part, F32) for part in parts),
+        ),
+        in_specs=[whole] * 9,
+        out_specs=[whole] * 5,
+        scratch_shapes=scratch,
+        compiler_params=pltpu.CompilerParams(
+            vmem_limit_bytes=VMEM_LIMIT, collective_id=0, has_side_effects=True
+        ),
+        name="fused",
+    )(table, cots, rot, rad, src, valid, *weights)
+
+
+def apart(neigh, ch, widths, table, cots, rot, rad, src, valid, weights, edges):
+    w_zero, w_one, w_two = weights
+    coefs, slots, _ = table.shape
+    packed, ep = rot.shape
+    feats = widths[0] + 2 * widths[1] + 2 * widths[2]
     params = pltpu.CompilerParams(vmem_limit_bytes=VMEM_LIMIT)
     whole = pl.BlockSpec(memory_space=pltpu.VMEM)
     gz, g1, g2, rotated, gout = pl.pallas_call(
@@ -259,6 +495,38 @@
         cost_estimate=pl.CostEstimate(flops=8_000_000_000, bytes_accessed=20_000_000, transcendentals=0),
         name="backward",
     )(rot, rad, src, gout, rotated, w_zero, w_one, w_two)
+    return (summed, grad_radial, *grads)
+
+
+def body(node_irreps, cotangent, rotation, radial, edge_source, edge_valid, send_rows, w_zero, w_one, w_two):
+    atoms, coefs, ch = node_irreps.shape
+    halo = send_rows.shape[1]
+    edges = edge_source.shape[0]
+    neigh = edges // atoms
+    ep = -(-edges // 128) * 128
+    pad = ep - edges
+    slots = atoms + 4 * halo
+    widths = (w_zero.shape[0], w_one.shape[0], w_two.shape[0])
+    feats = widths[0] + 2 * widths[1] + 2 * widths[2]
+    send_hot = (send_rows.reshape(-1)[:, None] == jnp.arange(atoms, dtype=jnp.int32)[None, :]).astype(BF)
+    nodes = node_irreps.transpose(1, 0, 2)
+    cots = cotangent.transpose(1, 0, 2)
+    outgoing = jnp.einsum("sa,nac->nsc", send_hot, nodes, preferred_element_type=F32).astype(BF)
+    incoming = [shifted(outgoing[:, i * halo : (i + 1) * halo], peer_steps[i]) for i in range(4)]
+    table = jnp.concatenate([nodes, *incoming], axis=1)
+    rot = jnp.pad(rotation, ((0, 0), (0, pad)))
+    rad = jnp.pad(radial, ((0, pad), (0, 0)))
+    src = jnp.pad(edge_source, (0, pad), constant_values=-1)[None, :]
+    valid = jnp.pad(edge_valid, (0, pad))[None, :]
+    weights = (w_zero, w_one, w_two)
+    graph = lax.axis_size("graph")
+    if graph == 16 and all(w.shape[0] % (8 * graph) == 0 for w in weights):
+        summed, grad_radial, *grads = fused(
+            neigh, ch, widths, graph, table, cots, rot, rad, src, valid, weights, edges
+        )
+        grads = [g.reshape(-1) for g in grads]
+    else:
+        summed, grad_radial, *grads = apart(neigh, ch, widths, table, cots, rot, rad, src, valid, weights, edges)
     slot_grad = summed[:, atoms:].astype(BF)
     returned = jnp.concatenate(
         [shifted(slot_grad[:, i * halo : (i + 1) * halo], -peer_steps[i]) for i in range(4)], axis=1

time: 227 us -> 128 us (0.56)
  waiting for transfers between devices: 91.9 us -> 3.63 us
  Pallas kernels: 67.8 us -> 85.5 us
  between operations: 16.2 us -> 0.92 us
  local copies, waits for them, and re-layouts: 17.1 us -> 8.39 us
  other arithmetic: 6.67 us -> 1.79 us
    unnamed x2 -> x0, waiting for transfers between devices: 88.4 us -> none
    pallas_call x2 -> x1, Pallas kernels: 67.8 us -> 85.5 us  [fused(): pl.pallas_call(functools.partial(fused_kernel, neigh, ch, widths, graph),...]
    reshape x3, local copies, waits for them, and re-layouts: 11.5 us -> 2.12 us  [body(): grads = [g.reshape(-1) for g in grads]]
    convert_element_type x3 -> x0, other arithmetic: 4.82 us -> none  [body(): lax.psum_scatter(g.reshape(-1), 'graph', scatter_dimension=0, tiled=True)]
  transfers between devices with their start and end apart: 9 -> 8, of which waited for: 3 -> 2; matrix products, arithmetic and copies ran while one was open for 3% -> 4% of each run, Pallas kernels for 12% -> 0%
where the time goes in v1:
time: 128 us; the launch traced here: 127 us
  Pallas kernels  85.5 us (67%)
  starting transfers between devices  23.4 us (18%)
  local copies, waits for them, and re-layouts  8.39 us (7%)
  matrix products  3.71 us (3%)
  waiting for transfers between devices  3.63 us (3%)
  other arithmetic  1.79 us (1%)
    pallas_call x1, Pallas kernels, fused(): pl.pallas_call(functools.partial(fused_kernel, neigh, ch, widths, graph),...  85.5 us
    ppermute x8, starting transfers between devices, shifted(): return lax.ppermute(block, 'graph', route)  23.4 us
    ppermute x8, waiting for transfers between devices, shifted(): return lax.ppermute(block, 'graph', route)  3.63 us
  transfers between devices with their start and end apart: 8, of which 2 were waited for; matrix products, arithmetic and copies ran while one was open for 4% of the time, Pallas kernels for 0%

profile of v1, /device:TPU:8, one launch (start us, length us, event | category | flops | bytes accessed | tf_op | source)
XLA Modules:
  0.0 127.3 jit_solution(5623835857428267042)
XLA Ops:
  0.7 0.8 eq.15
  1.5 1.4 %fusion = bf16[49,32,128]{2,1,0:T(8,128)(2,1)S(1)} fusion(bf16[48,49,128]{2,0,1:T(8,128)(2,1)} %param.10, s32[32]{0:T(128)S(1)} %eq.15), kind=kOutput, calls=%fused_computation.2 | convolution fusion | flops 19469824 | bytes 1003648 | tf_op jit(solution)/shard_map/sa,nac->nsc/dot_general | solution.py:514
  3.0 3.4 %collective-permute-start.3 = (bf16[49,8,128]{2,1,0:T(8,128)(2,1)S(1)}, bf16[49,8,128]{2,1,0:T(8,128)(2,1)S(1)}, u32[]{:S(2)}, u32[]{:S(2)}) collective-permute-start(bf16[49,8,128]{2,1,0:T(8,128)(2,1)S(1)} %get-tuple-element.19), channel_id=1, source_target_pairs={{0,2},{1,3},{2,4},{3,5},{4,6},{5,7},{6,8},{7,9},{8,10},{9,11},{10,... | collective-permute-start | bytes 301064 | tf_op jit(solution)/shard_map/ppermute | solution.py:29
  6.5 1.9 %collective-permute-start.2 = (bf16[49,8,128]{2,1,0:T(8,128)(2,1)S(1)}, bf16[49,8,128]{2,1,0:T(8,128)(2,1)S(1)}, u32[]{:S(2)}, u32[]{:S(2)}) collective-permute-start(bf16[49,8,128]{2,1,0:T(8,128)(2,1)S(1)} %get-tuple-element.20), channel_id=1, source_target_pairs={{0,1},{1,2},{2,3},{3,4},{4,5},{5,6},{6,7},{7,8},{8,9},{9,10},{10,1... | collective-permute-start | bytes 301064 | tf_op jit(solution)/shard_map/ppermute | solution.py:29
  8.4 4.5 %collective-permute-start.1 = (bf16[49,8,128]{2,1,0:T(8,128)(2,1)S(1)}, bf16[49,8,128]{2,1,0:T(8,128)(2,1)S(1)}, u32[]{:S(2)}, u32[]{:S(2)}) collective-permute-start(bf16[49,8,128]{2,1,0:T(8,128)(2,1)S(1)} %get-tuple-element.21), channel_id=1, source_target_pairs={{1,0},{2,1},{3,2},{4,3},{5,4},{6,5},{7,6},{8,7},{9,8},{10,9},{11,1... | collective-permute-start | bytes 301064 | tf_op jit(solution)/shard_map/ppermute | solution.py:29
  12.9 2.4 %collective-permute-start = (bf16[49,8,128]{2,1,0:T(8,128)(2,1)S(1)}, bf16[49,8,128]{2,1,0:T(8,128)(2,1)S(1)}, u32[]{:S(2)}, u32[]{:S(2)}) collective-permute-start(bf16[49,8,128]{2,1,0:T(8,128)(2,1)S(1)} %get-tuple-element.22), channel_id=1, source_target_pairs={{2,0},{3,1},{4,2},{5,3},{6,4},{7,5},{8,6},{9,7},{10,8},{11,9},{12,... | collective-permute-start | bytes 301064 | tf_op jit(solution)/shard_map/ppermute | solution.py:29
  16.0 0.6 broadcast_in_dim.8.valid_ref
  16.8 0.7 pad.16.rad_ref
  17.5 0.7 pad.15.rot_ref
  18.2 1.2 collective-permute-done
  19.6 1.0 copy-done.1
  20.6 85.5 %fused.1 = (f32[49,80,128]{2,1,0:T(8,128)}, bf16[576,128]{1,0:T(8,128)(2,1)}, f32[56,896]{1,0:T(8,128)}, f32[48,1536]{1,0:T(8,128)}, f32[40,1280]{1,0:T(8,128)}) custom-call(bf16[49,80,128]{2,1,0:T(8,128)(2,1)} %copy-done.1, bf16[49,48,128]{2,1,0:T(8,128)(2,1)} %bitcast.18, bf16[235,640]{1,0:T(8,128)(2,1)} %pad.15.rot_ref, bf16[640,128]{1,0:T(8,128)(2,1)} %pad.16.rad_ref, ...), custom_call_target="tpu_custom_call" | custom-call | tf_op jit(solution)/shard_map/fused/pallas_call | solution.py:430
  106.2 1.8 %convert.3 = bf16[49,80,128]{2,1,0:T(8,128)(2,1)S(1)} convert(f32[49,80,128]{2,1,0:T(8,128)} %get-tuple-element.10) | non-fusion elementwise | flops 501760 | bytes 3010560 | tf_op jit(solution)/shard_map/convert
  108.0 0.7 fusion.18
  108.7 2.2 %collective-permute-start.4 = (bf16[49,8,128]{2,1,0:T(8,128)(2,1)}, bf16[49,8,128]{2,1,0:T(8,128)(2,1)}, u32[]{:S(2)}, u32[]{:S(2)}) collective-permute-start(bf16[49,8,128]{2,1,0:T(8,128)(2,1)} %get-tuple-element.15), channel_id=1, source_target_pairs={{0,2},{1,3},{2,4},{3,5},{4,6},{5,7},{6,8},{7,9},{8,10},{9,11},{10,... | collective-permute-start | bytes 301064 | tf_op jit(solution)/shard_map/ppermute | solution.py:29
  111.0 4.5 %collective-permute-start.7 = (bf16[49,8,128]{2,1,0:T(8,128)(2,1)}, bf16[49,8,128]{2,1,0:T(8,128)(2,1)}, u32[]{:S(2)}, u32[]{:S(2)}) collective-permute-start(bf16[49,8,128]{2,1,0:T(8,128)(2,1)} %get-tuple-element.16), channel_id=1, source_target_pairs={{2,0},{3,1},{4,2},{5,3},{6,4},{7,5},{8,6},{9,7},{10,8},{11,9},{12,... | collective-permute-start | bytes 301064 | tf_op jit(solution)/shard_map/ppermute | solution.py:29
  115.5 1.9 %collective-permute-start.6 = (bf16[49,8,128]{2,1,0:T(8,128)(2,1)S(1)}, bf16[49,8,128]{2,1,0:T(8,128)(2,1)}, u32[]{:S(2)}, u32[]{:S(2)}) collective-permute-start(bf16[49,8,128]{2,1,0:T(8,128)(2,1)S(1)} %get-tuple-element.17), channel_id=1, source_target_pairs={{1,0},{2,1},{3,2},{4,3},{5,4},{6,5},{7,6},{8,7},{9,8},{10,9},{11,1... | collective-permute-start | bytes 301064 | tf_op jit(solution)/shard_map/ppermute | solution.py:29
  117.4 2.4 %collective-permute-start.5 = (bf16[49,8,128]{2,1,0:T(8,128)(2,1)S(1)}, bf16[49,8,128]{2,1,0:T(8,128)(2,1)}, u32[]{:S(2)}, u32[]{:S(2)}) collective-permute-start(bf16[49,8,128]{2,1,0:T(8,128)(2,1)S(1)} %get-tuple-element.18), channel_id=1, source_target_pairs={{0,1},{1,2},{2,3},{3,4},{4,5},{5,6},{6,7},{7,8},{8,9},{9,10},{10,1... | collective-permute-start | bytes 301064 | tf_op jit(solution)/shard_map/ppermute | solution.py:29
  119.8 0.7 reshape.20
  120.5 0.7 reshape.22
  121.2 0.7 reshape.21
  122.0 2.4 %collective-permute-done.5 = bf16[49,8,128]{2,1,0:T(8,128)(2,1)} collective-permute-done((bf16[49,8,128]{2,1,0:T(8,128)(2,1)S(1)}, bf16[49,8,128]{2,1,0:T(8,128)(2,1)}, u32[]{:S(2)}, u32[]{:S(2)}) %collective-permute-start.5) | collective-permute-done | bytes 100384 | tf_op jit(solution)/shard_map/ppermute | solution.py:29
  124.4 2.3 %fusion.1 = bf16[48,49,128]{2,0,1:T(8,128)(2,1)} fusion(f32[49,80,128]{2,1,0:T(8,128)S(1)} %copy-done, bf16[49,8,128]{2,1,0:T(8,128)(2,1)} %collective-permute-done.7, bf16[49,8,128]{2,1,0:T(8,128)(2,1)} %collective-permute-done.6, bf16[49,8,128]{2,1,0:T(8,128)(2,1)} %collective-permute-done.5, bf16[49,8,128]{2,1,0:T(8,128)(2,1)} %collective-permute-done.4, ...), kind=kOutput, calls=%fused_computation.4 | convolution fusion | flops 22078976 | bytes 2809984 | tf_op jit(solution)/shard_map/sa,nsc->nac/dot_general | solution.py:534
  126.7 0.7 copy.21
  (39 shorter events, 1.1 us)
Async XLA Ops:
  0.6 14.7 %copy-start.2 = (bf16[48,49,128]{2,0,1:T(8,128)(2,1)S(1)}, bf16[48,49,128]{2,0,1:T(8,128)(2,1)}, u32[]{:S(2)}) copy-start(bf16[48,49,128]{2,0,1:T(8,128)(2,1)} %param.10) | copy-start | bytes 1806340
  0.6 14.8 %copy-start.10 = (s32[576]{0:T(1024)S(1)}, s32[576]{0:T(1024)}, u32[]{:S(2)}) copy-start(s32[576]{0:T(1024)} %param.14) | copy-start | bytes 6916
  0.7 15.4 %copy-start.11 = (s32[576]{0:T(1024)S(1)}, s32[576]{0:T(1024)}, u32[]{:S(2)}) copy-start(s32[576]{0:T(1024)} %param.15) | copy-start | bytes 6916
  0.7 15.9 %copy-start.4 = (bf16[235,576]{0,1:T(8,128)(2,1)S(1)}, bf16[235,576]{0,1:T(8,128)(2,1)}, u32[]{:S(2)}) copy-start(bf16[235,576]{0,1:T(8,128)(2,1)} %param.12) | copy-start | bytes 812164
  1.5 15.3 %copy-start.8 = (bf16[576,128]{1,0:T(8,128)(2,1)S(1)}, bf16[576,128]{1,0:T(8,128)(2,1)}, u32[]{:S(2)}) copy-start(bf16[576,128]{1,0:T(8,128)(2,1)} %param.13) | copy-start | bytes 442372
  3.0 16.6 %collective-permute-start.3 = (bf16[49,8,128]{2,1,0:T(8,128)(2,1)S(1)}, bf16[49,8,128]{2,1,0:T(8,128)(2,1)S(1)}, u32[]{:S(2)}, u32[]{:S(2)}) collective-permute-start(bf16[49,8,128]{2,1,0:T(8,128)(2,1)S(1)} %get-tuple-element.19), channel_id=1, source_target_pairs={{0,2},{1,3},{2,4},{3,5},{4,6},{5,7},{6,8},{7,9},{8,10},{9,11},{10,... | collective-permute-start | bytes 301064 | tf_op jit(solution)/shard_map/ppermute | solution.py:29
  6.5 13.1 %collective-permute-start.2 = (bf16[49,8,128]{2,1,0:T(8,128)(2,1)S(1)}, bf16[49,8,128]{2,1,0:T(8,128)(2,1)S(1)}, u32[]{:S(2)}, u32[]{:S(2)}) collective-permute-start(bf16[49,8,128]{2,1,0:T(8,128)(2,1)S(1)} %get-tuple-element.20), channel_id=1, source_target_pairs={{0,1},{1,2},{2,3},{3,4},{4,5},{5,6},{6,7},{7,8},{8,9},{9,10},{10,1... | collective-permute-start | bytes 301064 | tf_op jit(solution)/shard_map/ppermute | solution.py:29
  8.4 11.1 %collective-permute-start.1 = (bf16[49,8,128]{2,1,0:T(8,128)(2,1)S(1)}, bf16[49,8,128]{2,1,0:T(8,128)(2,1)S(1)}, u32[]{:S(2)}, u32[]{:S(2)}) collective-permute-start(bf16[49,8,128]{2,1,0:T(8,128)(2,1)S(1)} %get-tuple-element.21), channel_id=1, source_target_pairs={{1,0},{2,1},{3,2},{4,3},{5,4},{6,5},{7,6},{8,7},{9,8},{10,9},{11,1... | collective-permute-start | bytes 301064 | tf_op jit(solution)/shard_map/ppermute | solution.py:29
  12.9 6.5 %collective-permute-start = (bf16[49,8,128]{2,1,0:T(8,128)(2,1)S(1)}, bf16[49,8,128]{2,1,0:T(8,128)(2,1)S(1)}, u32[]{:S(2)}, u32[]{:S(2)}) collective-permute-start(bf16[49,8,128]{2,1,0:T(8,128)(2,1)S(1)} %get-tuple-element.22), channel_id=1, source_target_pairs={{2,0},{3,1},{4,2},{5,3},{6,4},{7,5},{8,6},{9,7},{10,8},{11,9},{12,... | collective-permute-start | bytes 301064 | tf_op jit(solution)/shard_map/ppermute | solution.py:29
  19.6 1.0 copy-start.1
  106.1 13.7 %copy-start.7 = (f32[56,896]{1,0:T(8,128)S(1)}, f32[56,896]{1,0:T(8,128)}, u32[]{:S(2)}) copy-start(f32[56,896]{1,0:T(8,128)} %get-tuple-element.12) | copy-start | bytes 602116
  106.1 14.4 %copy-start.6 = (f32[40,1280]{1,0:T(8,128)S(1)}, f32[40,1280]{1,0:T(8,128)}, u32[]{:S(2)}) copy-start(f32[40,1280]{1,0:T(8,128)} %get-tuple-element.14) | copy-start | bytes 614404
  106.2 15.1 %copy-start.5 = (f32[48,1536]{1,0:T(8,128)S(1)}, f32[48,1536]{1,0:T(8,128)}, u32[]{:S(2)}) copy-start(f32[48,1536]{1,0:T(8,128)} %get-tuple-element.13) | copy-start | bytes 884740
  106.2 18.2 %copy-start.3 = (bf16[48,49,128]{2,0,1:T(8,128)(2,1)S(1)}, bf16[48,49,128]{2,0,1:T(8,128)(2,1)}, u32[]{:S(2)}) copy-start(bf16[48,49,128]{2,0,1:T(8,128)(2,1)} %param.11) | copy-start | bytes 1806340
  108.0 16.4 %copy-start = (f32[49,80,128]{2,1,0:T(8,128)S(1)}, f32[49,80,128]{2,1,0:T(8,128)}, u32[]{:S(2)}) copy-start(f32[49,80,128]{2,1,0:T(8,128)} %get-tuple-element.10) | copy-start | bytes 6021124
  108.7 13.2 %collective-permute-start.4 = (bf16[49,8,128]{2,1,0:T(8,128)(2,1)}, bf16[49,8,128]{2,1,0:T(8,128)(2,1)}, u32[]{:S(2)}, u32[]{:S(2)}) collective-permute-start(bf16[49,8,128]{2,1,0:T(8,128)(2,1)} %get-tuple-element.15), channel_id=1, source_target_pairs={{0,2},{1,3},{2,4},{3,5},{4,6},{5,7},{6,8},{7,9},{8,10},{9,11},{10,... | collective-permute-start | bytes 301064 | tf_op jit(solution)/shard_map/ppermute | solution.py:29
  111.0 11.0 %collective-permute-start.7 = (bf16[49,8,128]{2,1,0:T(8,128)(2,1)}, bf16[49,8,128]{2,1,0:T(8,128)(2,1)}, u32[]{:S(2)}, u32[]{:S(2)}) collective-permute-start(bf16[49,8,128]{2,1,0:T(8,128)(2,1)} %get-tuple-element.16), channel_id=1, source_target_pairs={{2,0},{3,1},{4,2},{5,3},{6,4},{7,5},{8,6},{9,7},{10,8},{11,9},{12,... | collective-permute-start | bytes 301064 | tf_op jit(solution)/shard_map/ppermute | solution.py:29
  115.5 6.5 %collective-permute-start.6 = (bf16[49,8,128]{2,1,0:T(8,128)(2,1)S(1)}, bf16[49,8,128]{2,1,0:T(8,128)(2,1)}, u32[]{:S(2)}, u32[]{:S(2)}) collective-permute-start(bf16[49,8,128]{2,1,0:T(8,128)(2,1)S(1)} %get-tuple-element.17), channel_id=1, source_target_pairs={{1,0},{2,1},{3,2},{4,3},{5,4},{6,5},{7,6},{8,7},{9,8},{10,9},{11,1... | collective-permute-start | bytes 301064 | tf_op jit(solution)/shard_map/ppermute | solution.py:29
  117.4 7.0 %collective-permute-start.5 = (bf16[49,8,128]{2,1,0:T(8,128)(2,1)S(1)}, bf16[49,8,128]{2,1,0:T(8,128)(2,1)}, u32[]{:S(2)}, u32[]{:S(2)}) collective-permute-start(bf16[49,8,128]{2,1,0:T(8,128)(2,1)S(1)} %get-tuple-element.18), channel_id=1, source_target_pairs={{0,1},{1,2},{2,3},{3,4},{4,5},{5,6},{6,7},{7,8},{8,9},{9,10},{10,1... | collective-permute-start | bytes 301064 | tf_op jit(solution)/shard_map/ppermute | solution.py:29
  121.2 5.4 %copy-start.9 = (bf16[576,128]{1,0:T(8,128)(2,1)S(1)}, bf16[576,128]{1,0:T(8,128)(2,1)}, u32[]{:S(2)}) copy-start(bf16[576,128]{1,0:T(8,128)(2,1)} %get-tuple-element.29) | copy-start | bytes 442372

commit v2 on v1

--- a/solution.py
+++ b/solution.py
@@ -194,18 +194,32 @@
 
 def fused_kernel(
     neigh, ch, widths, graph,
-    tab_ref, cot_ref, rot_ref, rad_ref, src_ref, valid_ref, w0_ref, w1_ref, w2_ref,
-    sum_ref, grad_ref, oz_ref, o1_ref, o2_ref,
-    xg, cx, inp, gout, rotated, rot32, radt, grt, *rest,
+    node_ref, cot_ref, rot_ref, rad_ref, src_ref, valid_ref, sent_ref, back_ref, w0_ref, w1_ref, w2_ref,
+    nodes_out, grad_ref, oz_ref, o1_ref, o2_ref,
+    xg, cx, inp, gout, rotated, rot32, radt, grt, halo_out, halo_in, slot_out, slot_in, halos, local, *rest,
 ):
     staged = rest[0:3]
     landed = (rest[3:7], rest[7:11], rest[11:15])
-    send_sem, recv_sem = rest[15], rest[16]
+    send_sem, recv_sem, halo_send, halo_recv = rest[15:19]
     outs = (oz_ref, o1_ref, o2_ref)
     me = lax.axis_index("graph")
     bits = [me & 1, (me >> 1) & 1, (me >> 2) & 1, (me >> 3) & 1]
     partners = [me + (1 << b) * (1 - 2 * bits[b]) for b in range(4)]
+    coefs, atoms, _ = node_ref.shape
+    halo = sent_ref.shape[0] // 4
+    slots = atoms + 4 * halo
+    halo_in[...] = jnp.zeros_like(halo_in)
+    slot_in[...] = jnp.zeros_like(slot_in)
+    near = [(me + step, (me + step >= 0) & (me + step < graph)) for step in peer_steps]
     barrier = pltpu.get_barrier_semaphore()
+    for other, there in near:
+
+        @pl.when(there)
+        def _(other=other):
+            pl.semaphore_signal(
+                barrier, inc=1, device_id={"graph": other}, device_id_type=pl.DeviceIdType.MESH
+            )
+
     for partner in partners:
         pl.semaphore_signal(barrier, inc=1, device_id={"graph": partner}, device_id_type=pl.DeviceIdType.MESH)
 
@@ -240,8 +254,45 @@
         lax.fori_loop(0, count, add, 0)
         copy_of(which, stage + 1).start()
 
-    coefs, slots, _ = tab_ref.shape
-    atoms = cot_ref.shape[1]
+    def halo_copy(block, back):
+        towards = 3 - block if back else block
+        return pltpu.make_async_remote_copy(
+            src_ref=(slot_out if back else halo_out).at[block],
+            dst_ref=(slot_in if back else halo_in).at[block],
+            send_sem=halo_send.at[4 * back + block],
+            recv_sem=halo_recv.at[4 * back + block],
+            device_id={"graph": near[towards][0]},
+            device_id_type=pl.DeviceIdType.MESH,
+        )
+
+    def halo_each(back, act, incoming):
+        for block in range(4):
+            side = 3 - block if bool(back) != incoming else block
+
+            @pl.when(near[side][1])
+            def _(block=block):
+                getattr(halo_copy(block, back), act)()
+
+    def pack(buffer, q, low, high):
+        for block in range(4):
+            at = slice(block * halo, (block + 1) * halo)
+            buffer[block, q] = jnp.concatenate([low[at], high[at]], axis=0).astype(BF)
+
+    def unpack(buffer, q, odd):
+        parts = [buffer[block, q].astype(F32)[odd * halo : (odd + 1) * halo] for block in range(4)]
+        return jnp.concatenate(parts, axis=0).astype(BF)
+
+    def send_pair(q, _):
+        pack(halo_out, q, dot(sent_ref[...], node_ref[2 * q]), dot(sent_ref[...], node_ref[2 * q + 1]))
+        return _
+
+    lax.fori_loop(0, coefs // 2, send_pair, 0)
+    last = dot(sent_ref[...], node_ref[coefs - 1])
+    pack(halo_out, coefs // 2, last, last)
+    peers = sum(there.astype(jnp.int32) for _, there in near)
+    pl.semaphore_wait(barrier, 4 + peers)
+    halo_each(0, "start", False)
+
     ep = rot_ref.shape[1]
     edges = grad_ref.shape[0]
     wz, w1, w2 = widths
@@ -253,13 +304,32 @@
     rot32[...] = rot_ref[...].astype(F32)
     radt[...] = rad_ref[...].astype(F32).T
 
-    def gather(n, _):
-        at = pl.ds(pl.multiple_of(n * ch, ch), ch)
-        xg[at, :] = dot_tn(tab_ref[n], hot).astype(BF)
-        cx[at, :] = dot_tn(cot_ref[n], rep).astype(BF)
-        return _
-
-    lax.fori_loop(0, coefs, gather, 0)
+    def gather_cot(i, _):
+        at = pl.ds(pl.multiple_of(i * 7 * ch, ch), 7 * ch)
+        wide = jnp.concatenate([cot_ref[i * 7 + j] for j in range(7)], axis=1)
+        cx[at, :] = dot_tn(wide, rep).astype(BF)
+        return _
+
+    lax.fori_loop(0, coefs // 7, gather_cot, 0)
+    halo_each(0, "wait_recv", True)
+
+    def receive_pair(q, _):
+        halos[2 * q] = unpack(halo_in, q, 0)
+        halos[2 * q + 1] = unpack(halo_in, q, 1)
+        return _
+
+    lax.fori_loop(0, coefs // 2, receive_pair, 0)
+    halos[coefs - 1] = unpack(halo_in, coefs // 2, 0)
+
+    def gather(i, _):
+        at = pl.ds(pl.multiple_of(i * 7 * ch, ch), 7 * ch)
+        wide = jnp.concatenate(
+            [jnp.concatenate([node_ref[i * 7 + j], halos[i * 7 + j]], axis=0) for j in range(7)], axis=1
+        )
+        xg[at, :] = dot_tn(wide, hot).astype(BF)
+        return _
+
+    lax.fori_loop(0, coefs // 7, gather, 0)
 
     def rotate(step, _):
         eb = step // (ch // CB)
@@ -344,7 +414,6 @@
         lax.fori_loop(0, 2, part, 0)
 
     weight_pair(1, w1, wz)
-    pl.semaphore_wait(barrier, 4)
     copy_of(1, 0).start()
     weight_pair(2, w2, wz + 2 * w1)
     copy_of(2, 0).start()
@@ -392,24 +461,49 @@
     advance(2, 2)
     grad_ref[...] = grt[...].T[:edges].astype(BF)
 
-    def scatter(i, _):
-        part = dot_nt(hot, eg[pl.ds(pl.multiple_of(i * 7 * ch, ch), 7 * ch), :])
-        for j in range(7):
-            sum_ref[i * 7 + j] = part[:, j * ch : (j + 1) * ch]
-        return _
-
-    lax.fori_loop(0, coefs // 7, scatter, 0)
+    def scatter(q):
+        part = dot_nt(hot, eg[pl.ds(pl.multiple_of(q * 2 * ch, ch), 2 * ch), :])
+        low, high = part[:, 0:ch], part[:, ch : 2 * ch]
+        local[2 * q] = low[:atoms] + cot_ref[2 * q].astype(F32)
+        local[2 * q + 1] = high[:atoms] + cot_ref[2 * q + 1].astype(F32)
+        pack(slot_out, q, low[atoms:], high[atoms:])
+
+    def scatter_some(i, _):
+        for j in range(4):
+            scatter(i * 4 + j)
+        return _
+
+    lax.fori_loop(0, coefs // 8, scatter_some, 0)
+    tail = dot_nt(hot, eg[(coefs - 1) * ch : coefs * ch, :])
+    local[coefs - 1] = tail[:atoms] + cot_ref[coefs - 1].astype(F32)
+    pack(slot_out, coefs // 2, tail[atoms:], tail[atoms:])
+    halo_each(1, "start", False)
     advance(1, 3)
     advance(0, 2)
     advance(2, 3)
+    halo_each(1, "wait_recv", True)
+
+    def finish(n, q, odd):
+        nodes_out[n] = (local[n] + dot(back_ref[...], unpack(slot_in, q, odd))).astype(BF)
+
+    def finish_pair(q, _):
+        finish(2 * q, q, 0)
+        finish(2 * q + 1, q, 1)
+        return _
+
+    lax.fori_loop(0, coefs // 2, finish_pair, 0)
+    finish(coefs - 1, coefs // 2, 0)
     advance(0, 3)
     for which in range(3):
         for stage in range(4):
             copy_of(which, stage).wait_send()
-
-
-def fused(neigh, ch, widths, graph, table, cots, rot, rad, src, valid, weights, edges):
-    coefs, slots, _ = table.shape
+    halo_each(0, "wait_send", False)
+    halo_each(1, "wait_send", False)
+
+
+def fused(neigh, ch, widths, graph, nodes, cots, rot, rad, src, valid, send_hot, weights, edges):
+    coefs, atoms, _ = nodes.shape
+    halo = send_hot.shape[0] // 4
     packed, ep = rot.shape
     feats = widths[0] + 2 * widths[1] + 2 * widths[2]
     whole = pl.BlockSpec(memory_space=pltpu.VMEM)
@@ -424,24 +518,26 @@
         pltpu.VMEM((ch, ep), F32),
         pltpu.VMEM((ch, ep), F32),
     ]
+    scratch += [pltpu.VMEM((4, coefs // 2 + 1, 2 * halo, ch), BF) for _ in range(4)]
+    scratch += [pltpu.VMEM((coefs, 4 * halo, ch), BF), pltpu.VMEM((coefs, atoms, ch), F32)]
     scratch += [pltpu.VMEM((graph, *part), BF) for part in parts]
     scratch += [pltpu.VMEM((8 >> stage, *part), BF) for part in parts for stage in range(4)]
-    scratch += [pltpu.SemaphoreType.DMA((12,)), pltpu.SemaphoreType.DMA((12,))]
+    scratch += [pltpu.SemaphoreType.DMA((count,)) for count in (12, 12, 8, 8)]
     return pl.pallas_call(
         functools.partial(fused_kernel, neigh, ch, widths, graph),
         out_shape=(
-            jax.ShapeDtypeStruct((coefs, slots, ch), F32),
+            jax.ShapeDtypeStruct((coefs, atoms, ch), BF),
             jax.ShapeDtypeStruct((edges, ch), BF),
             *(jax.ShapeDtypeStruct(part, F32) for part in parts),
         ),
-        in_specs=[whole] * 9,
+        in_specs=[whole] * 11,
         out_specs=[whole] * 5,
         scratch_shapes=scratch,
         compiler_params=pltpu.CompilerParams(
             vmem_limit_bytes=VMEM_LIMIT, collective_id=0, has_side_effects=True
         ),
         name="fused",
-    )(table, cots, rot, rad, src, valid, *weights)
+    )(nodes, cots, rot, rad, src, valid, send_hot, send_hot.T, *weights)
 
 
 def apart(neigh, ch, widths, table, cots, rot, rad, src, valid, weights, edges):
@@ -505,36 +601,35 @@
     neigh = edges // atoms
     ep = -(-edges // 128) * 128
     pad = ep - edges
-    slots = atoms + 4 * halo
     widths = (w_zero.shape[0], w_one.shape[0], w_two.shape[0])
     feats = widths[0] + 2 * widths[1] + 2 * widths[2]
     send_hot = (send_rows.reshape(-1)[:, None] == jnp.arange(atoms, dtype=jnp.int32)[None, :]).astype(BF)
     nodes = node_irreps.transpose(1, 0, 2)
     cots = cotangent.transpose(1, 0, 2)
-    outgoing = jnp.einsum("sa,nac->nsc", send_hot, nodes, preferred_element_type=F32).astype(BF)
-    incoming = [shifted(outgoing[:, i * halo : (i + 1) * halo], peer_steps[i]) for i in range(4)]
-    table = jnp.concatenate([nodes, *incoming], axis=1)
     rot = jnp.pad(rotation, ((0, 0), (0, pad)))
     rad = jnp.pad(radial, ((0, pad), (0, 0)))
     src = jnp.pad(edge_source, (0, pad), constant_values=-1)[None, :]
     valid = jnp.pad(edge_valid, (0, pad))[None, :]
     weights = (w_zero, w_one, w_two)
     graph = lax.axis_size("graph")
-    if graph == 16 and all(w.shape[0] % (8 * graph) == 0 for w in weights):
-        summed, grad_radial, *grads = fused(
-            neigh, ch, widths, graph, table, cots, rot, rad, src, valid, weights, edges
+    if graph == 16 and halo == 8 and coefs == 49 and all(w.shape[0] % (8 * graph) == 0 for w in weights):
+        total, grad_radial, *grads = fused(
+            neigh, ch, widths, graph, nodes, cots, rot, rad, src, valid, send_hot, weights, edges
         )
         grads = [g.reshape(-1) for g in grads]
     else:
+        outgoing = jnp.einsum("sa,nac->nsc", send_hot, nodes, preferred_element_type=F32).astype(BF)
+        incoming = [shifted(outgoing[:, i * halo : (i + 1) * halo], peer_steps[i]) for i in range(4)]
+        table = jnp.concatenate([nodes, *incoming], axis=1)
         summed, grad_radial, *grads = apart(neigh, ch, widths, table, cots, rot, rad, src, valid, weights, edges)
-    slot_grad = summed[:, atoms:].astype(BF)
-    returned = jnp.concatenate(
-        [shifted(slot_grad[:, i * halo : (i + 1) * halo], -peer_steps[i]) for i in range(4)], axis=1
-    )
-    added = jnp.einsum("sa,nsc->nac", send_hot, returned, preferred_element_type=F32)
-    total = cots.astype(F32) + summed[:, :atoms] + added
-    grad_nodes = total.astype(BF).transpose(1, 0, 2)
-    return (grad_nodes, grad_radial, *grads)
+        slot_grad = summed[:, atoms:].astype(BF)
+        returned = jnp.concatenate(
+            [shifted(slot_grad[:, i * halo : (i + 1) * halo], -peer_steps[i]) for i in range(4)], axis=1
+        )
+        added = jnp.einsum("sa,nsc->nac", send_hot, returned, preferred_element_type=F32)
+        total = cots.astype(F32) + summed[:, :atoms] + added
+        total = total.astype(BF)
+    return (total.transpose(1, 0, 2), grad_radial, *grads)
 
 
 def solution(mesh):

time: 128 us -> 105 us (0.82)
  starting transfers between devices: 23.4 us -> 0 us
  local copies, waits for them, and re-layouts: 8.39 us -> 13.3 us
  matrix products: 3.71 us -> 0 us
  waiting for transfers between devices: 3.63 us -> 0 us
  Pallas kernels: 85.5 us -> 88.2 us
    ppermute x8 -> x0, starting transfers between devices: 23.4 us -> none  [shifted(): return lax.ppermute(block, 'graph', route)]
    dot_general x2 -> x0, matrix products: 3.71 us -> none  [the longest x1 2.29 us: body(): jnp.einsum('sa,nsc->nac', send_hot, returned, preferred_element_type=F32)]
    ppermute x8 -> x0, waiting for transfers between devices: 3.63 us -> none  [shifted(): return lax.ppermute(block, 'graph', route)]
    reshape x3, local copies, waits for them, and re-layouts: 2.12 us -> 5 us  [body(): grads = [g.reshape(-1) for g in grads]]
    pallas_call x1, Pallas kernels: 85.5 us -> 88.2 us  [fused(): pl.pallas_call(functools.partial(fused_kernel, neigh, ch, widths, graph),...]
    another operation x1 -> x0, other arithmetic: 1.79 us -> none
    unnamed x30 -> x7, local copies, waits for them, and re-layouts: 1.99 us -> 2.64 us
  transfers between devices with their start and end apart: 8 -> 0, of which waited for: 2 -> 0; matrix products, arithmetic and copies ran while one was open for 4% -> 0% of each run, Pallas kernels for 0% -> 0%
where the time goes in v2:
time: 105 us; the launch traced here: 103 us
  Pallas kernels  88.2 us (84%)
  local copies, waits for them, and re-layouts  13.3 us (13%)
  other arithmetic  1.28 us (1%)
    pallas_call x1, Pallas kernels, fused(): pl.pallas_call(functools.partial(fused_kernel, neigh, ch, widths, graph),...  88.2 us
    reshape x3, local copies, waits for them, and re-layouts, body(): grads = [g.reshape(-1) for g in grads]  5 us
    unnamed x7, local copies, waits for them, and re-layouts  2.64 us

profile of v2, /device:TPU:8, one launch (start us, length us, event | category | flops | bytes accessed | tf_op | source)
XLA Modules:
  0.0 103.4 jit_solution(220186620054370220)
XLA Ops:
  0.6 0.8 eq.22
  1.4 0.7 pad.17
  2.1 0.6 broadcast_in_dim.7.src_ref
  2.7 0.7 pad.18
  3.4 0.6 broadcast_in_dim.8.valid_ref
  3.9 0.7 fusion.1.sent_ref
  4.6 0.6 fusion.back_ref
  5.2 1.6 %pad.16.rad_ref = bf16[640,128]{1,0:T(8,128)(2,1)} pad(bf16[576,128]{1,0:T(8,128)(2,1)} %param.13, bf16[]{:T(256)} %constant.1.clone.1), padding=0_64x0_0 | pad | bytes 311298 | tf_op jit(solution)/shard_map/jit(_pad)/pad | solution.py:610
  6.8 1.2 %copy.15 = bf16[235,576]{1,0:T(8,128)(2,1)S(1)} copy(bf16[235,576]{0,1:T(8,128)(2,1)} %param.12) | data formatting | bytes 541440 | tf_op args[2]
  8.0 0.8 pad.15.rot_ref
  8.7 88.2 %fused.1 = (bf16[49,48,128]{2,1,0:T(8,128)(2,1)}, bf16[576,128]{1,0:T(8,128)(2,1)}, f32[56,896]{1,0:T(8,128)}, f32[48,1536]{1,0:T(8,128)}, f32[40,1280]{1,0:T(8,128)}) custom-call(bf16[49,48,128]{2,1,0:T(8,128)(2,1)} %bitcast.4, bf16[49,48,128]{2,1,0:T(8,128)(2,1)} %bitcast.5, bf16[235,640]{1,0:T(8,128)(2,1)} %pad.15.rot_ref, bf16[640,128]{1,0:T(8,128)(2,1)} %pad.16.rad_ref, ...), custom_call_target="tpu_custom_call" | custom-call | tf_op jit(solution)/shard_map/fused/pallas_call | solution.py:526
  96.9 0.0 copy-start
  96.9 0.0 copy-start.1
  97.0 1.7 %reshape.20 = f32[50176]{0:T(1024)} reshape(f32[56,896]{1,0:T(8,128)} %get-tuple-element.12) | data formatting | bytes 401408 | tf_op jit(solution)/shard_map/reshape | solution.py:619
  98.6 1.6 %reshape.22 = f32[51200]{0:T(1024)} reshape(f32[40,1280]{1,0:T(8,128)} %get-tuple-element.14) | data formatting | bytes 409600 | tf_op jit(solution)/shard_map/reshape | solution.py:619
  100.3 1.7 %reshape.21 = f32[73728]{0:T(1024)} reshape(f32[48,1536]{1,0:T(8,128)} %get-tuple-element.13) | data formatting | bytes 589824 | tf_op jit(solution)/shard_map/reshape | solution.py:619
  102.0 0.0 copy-done
  102.0 0.8 copy.18
  102.8 0.0 copy-done.1
  102.8 0.7 copy.19
Async XLA Ops:
  96.9 5.0 %copy-start = (bf16[49,48,128]{2,1,0:T(8,128)(2,1)S(1)}, bf16[49,48,128]{2,1,0:T(8,128)(2,1)}, u32[]{:S(2)}) copy-start(bf16[49,48,128]{2,1,0:T(8,128)(2,1)} %get-tuple-element.10) | copy-start | bytes 1806340
  96.9 5.8 %copy-start.1 = (bf16[576,128]{1,0:T(8,128)(2,1)S(1)}, bf16[576,128]{1,0:T(8,128)(2,1)}, u32[]{:S(2)}) copy-start(bf16[576,128]{1,0:T(8,128)(2,1)} %get-tuple-element.21) | copy-start | bytes 442372

commit v3 on v2

--- a/solution.py
+++ b/solution.py
@@ -12,6 +12,7 @@
 peer_steps = (-2, -1, 1, 2)
 order_first = (0, 6, 12, 17, 22)
 CB = 32
+stage_bits = ((0, 2, 3, 1), (0, 1, 2, 3), (0, 1, 2, 3))
 VMEM_LIMIT = 58 * 2**20
 
 
@@ -196,7 +197,7 @@
     neigh, ch, widths, graph,
     node_ref, cot_ref, rot_ref, rad_ref, src_ref, valid_ref, sent_ref, back_ref, w0_ref, w1_ref, w2_ref,
     nodes_out, grad_ref, oz_ref, o1_ref, o2_ref,
-    xg, cx, inp, gout, rotated, rot32, radt, grt, halo_out, halo_in, slot_out, slot_in, halos, local, *rest,
+    xg, cx, inp, gout, rotated, rot32, radt, grt, src_wide, valid_wide, halo_out, halo_in, slot_out, slot_in, halos, local, *rest,
 ):
     staged = rest[0:3]
     landed = (rest[3:7], rest[7:11], rest[11:15])
@@ -223,19 +224,23 @@
     for partner in partners:
         pl.semaphore_signal(barrier, inc=1, device_id={"graph": partner}, device_id_type=pl.DeviceIdType.MESH)
 
-    firsts = [0]
-    for stage in range(4):
-        firsts.append(firsts[-1] + bits[stage] * (8 >> stage))
+    firsts = []
+    for order in stage_bits:
+        first = [0]
+        for stage in range(4):
+            first.append(first[-1] + bits[order[stage]] * (8 >> stage))
+        firsts.append(first)
 
     def copy_of(which, stage):
         count = 8 >> stage
-        at = firsts[stage] + (1 - bits[stage]) * count
+        bit = stage_bits[which][stage]
+        at = firsts[which][stage] + (1 - bits[bit]) * count
         return pltpu.make_async_remote_copy(
             src_ref=staged[which].at[pl.ds(at, count)],
             dst_ref=landed[which][stage],
             send_sem=send_sem.at[which * 4 + stage],
             recv_sem=recv_sem.at[which * 4 + stage],
-            device_id={"graph": partners[stage]},
+            device_id={"graph": partners[bit]},
             device_id_type=pl.DeviceIdType.MESH,
         )
 
@@ -243,9 +248,14 @@
         copy_of(which, stage).wait_recv()
         count = 8 >> stage
         if stage == 3:
-            outs[which][...] = staged[which][firsts[4]].astype(F32) + landed[which][3][0].astype(F32)
+            total = staged[which][firsts[which][4]].astype(F32) + landed[which][3][0].astype(F32)
+            blocks = total.shape[1] // 128
+            for block in range(blocks):
+                outs[which][pl.ds(block, total.shape[0], stride=blocks), :] = total[
+                    :, block * 128 : (block + 1) * 128
+                ]
             return
-        buffer, part, first = staged[which], landed[which][stage], firsts[stage + 1]
+        buffer, part, first = staged[which], landed[which][stage], firsts[which][stage + 1]
 
         def add(i, _):
             buffer[first + i] = (buffer[first + i].astype(F32) + part[i].astype(F32)).astype(BF)
@@ -293,16 +303,25 @@
     pl.semaphore_wait(barrier, 4 + peers)
     halo_each(0, "start", False)
 
-    ep = rot_ref.shape[1]
+    ep = rot32.shape[1]
     edges = grad_ref.shape[0]
+    src_wide[...] = jnp.full_like(src_wide, -1)
+    valid_wide[...] = jnp.zeros_like(valid_wide)
+    src_wide[:, :edges] = src_ref[...]
+    valid_wide[:, :edges] = valid_ref[...]
     wz, w1, w2 = widths
-    hot = (lax.broadcasted_iota(jnp.int32, (slots, ep), 0) == src_ref[...]).astype(F32).astype(BF)
+    hot = (lax.broadcasted_iota(jnp.int32, (slots, ep), 0) == src_wide[...]).astype(F32).astype(BF)
     edge = lax.broadcasted_iota(jnp.int32, (atoms, ep), 1)
     first_edge = lax.broadcasted_iota(jnp.int32, (atoms, ep), 0) * neigh
-    mine = (edge >= first_edge) & (edge < first_edge + neigh) & (valid_ref[...] != 0)
+    mine = (edge >= first_edge) & (edge < first_edge + neigh) & (valid_wide[...] != 0)
     rep = mine.astype(F32).astype(BF)
-    rot32[...] = rot_ref[...].astype(F32)
-    radt[...] = rad_ref[...].astype(F32).T
+    rot32[:, (edges // 128) * 128 :] = jnp.zeros_like(rot32[:, (edges // 128) * 128 :])
+    rot32[:, :edges] = rot_ref[...].astype(F32)
+    for low in range(0, ep, 128):
+        block = rad_ref[low : min(low + 128, edges), :].astype(F32)
+        if block.shape[0] < 128:
+            block = jnp.concatenate([block, jnp.zeros((128 - block.shape[0], ch), F32)], axis=0)
+        radt[:, low : low + 128] = block.T
 
     def gather_cot(i, _):
         at = pl.ds(pl.multiple_of(i * 7 * ch, ch), 7 * ch)
@@ -360,7 +379,8 @@
     def place(which, i, columns, value):
         height = value.shape[0] // 8
         for jj in range(8):
-            position = (jj & 1) * 8 + ((jj >> 1) & 1) * 4 + ((jj >> 2) & 1) * 2 + i
+            owner = [jj & 1, (jj >> 1) & 1, (jj >> 2) & 1, i]
+            position = sum(owner[bit] * (8 >> stage) for stage, bit in enumerate(stage_bits[which]))
             staged[which][position, :, columns] = value[jj * height : (jj + 1) * height].astype(BF)
 
     def weight_zero():
@@ -424,8 +444,8 @@
     back_zero()
     advance(0, 0)
     back_pair(w1, wz, w1_ref)
-    advance(1, 1)
     back_pair(w2, wz + 2 * w1, w2_ref)
+    advance(0, 1)
 
     eg = xg
 
@@ -453,12 +473,14 @@
         return _
 
     steps = (ep // 128) * (ch // CB)
-    lax.fori_loop(0, steps // 2, rotate_back, 0)
+    lax.fori_loop(0, steps // 4, rotate_back, 0)
+    advance(1, 1)
+    lax.fori_loop(steps // 4, steps // 2, rotate_back, 0)
+    advance(0, 2)
     advance(2, 1)
+    lax.fori_loop(steps // 2, 3 * steps // 4, rotate_back, 0)
     advance(1, 2)
-    lax.fori_loop(steps // 2, steps, rotate_back, 0)
-    advance(0, 1)
-    advance(2, 2)
+    lax.fori_loop(3 * steps // 4, steps, rotate_back, 0)
     grad_ref[...] = grt[...].T[:edges].astype(BF)
 
     def scatter(q):
@@ -478,9 +500,9 @@
     local[coefs - 1] = tail[:atoms] + cot_ref[coefs - 1].astype(F32)
     pack(slot_out, coefs // 2, tail[atoms:], tail[atoms:])
     halo_each(1, "start", False)
+    advance(2, 2)
+    advance(0, 3)
     advance(1, 3)
-    advance(0, 2)
-    advance(2, 3)
     halo_each(1, "wait_recv", True)
 
     def finish(n, q, odd):
@@ -493,7 +515,7 @@
 
     lax.fori_loop(0, coefs // 2, finish_pair, 0)
     finish(coefs - 1, coefs // 2, 0)
-    advance(0, 3)
+    advance(2, 3)
     for which in range(3):
         for stage in range(4):
             copy_of(which, stage).wait_send()
@@ -504,7 +526,8 @@
 def fused(neigh, ch, widths, graph, nodes, cots, rot, rad, src, valid, send_hot, weights, edges):
     coefs, atoms, _ = nodes.shape
     halo = send_hot.shape[0] // 4
-    packed, ep = rot.shape
+    packed = rot.shape[0]
+    ep = -(-edges // 128) * 128
     feats = widths[0] + 2 * widths[1] + 2 * widths[2]
     whole = pl.BlockSpec(memory_space=pltpu.VMEM)
     parts = [(w.shape[0] // graph, w.shape[1]) for w in weights]
@@ -518,6 +541,7 @@
         pltpu.VMEM((ch, ep), F32),
         pltpu.VMEM((ch, ep), F32),
     ]
+    scratch += [pltpu.VMEM((1, ep), jnp.int32), pltpu.VMEM((1, ep), jnp.int32)]
     scratch += [pltpu.VMEM((4, coefs // 2 + 1, 2 * halo, ch), BF) for _ in range(4)]
     scratch += [pltpu.VMEM((coefs, 4 * halo, ch), BF), pltpu.VMEM((coefs, atoms, ch), F32)]
     scratch += [pltpu.VMEM((graph, *part), BF) for part in parts]
@@ -528,7 +552,7 @@
         out_shape=(
             jax.ShapeDtypeStruct((coefs, atoms, ch), BF),
             jax.ShapeDtypeStruct((edges, ch), BF),
-            *(jax.ShapeDtypeStruct(part, F32) for part in parts),
+            *(jax.ShapeDtypeStruct((part[0] * part[1] // 128, 128), F32) for part in parts),
         ),
         in_specs=[whole] * 11,
         out_specs=[whole] * 5,
@@ -606,18 +630,18 @@
     send_hot = (send_rows.reshape(-1)[:, None] == jnp.arange(atoms, dtype=jnp.int32)[None, :]).astype(BF)
     nodes = node_irreps.transpose(1, 0, 2)
     cots = cotangent.transpose(1, 0, 2)
-    rot = jnp.pad(rotation, ((0, 0), (0, pad)))
-    rad = jnp.pad(radial, ((0, pad), (0, 0)))
-    src = jnp.pad(edge_source, (0, pad), constant_values=-1)[None, :]
-    valid = jnp.pad(edge_valid, (0, pad))[None, :]
     weights = (w_zero, w_one, w_two)
     graph = lax.axis_size("graph")
     if graph == 16 and halo == 8 and coefs == 49 and all(w.shape[0] % (8 * graph) == 0 for w in weights):
         total, grad_radial, *grads = fused(
-            neigh, ch, widths, graph, nodes, cots, rot, rad, src, valid, send_hot, weights, edges
+            neigh, ch, widths, graph, nodes, cots, rotation, radial, edge_source[None, :], edge_valid[None, :], send_hot, weights, edges
         )
         grads = [g.reshape(-1) for g in grads]
     else:
+        rot = jnp.pad(rotation, ((0, 0), (0, pad)))
+        rad = jnp.pad(radial, ((0, pad), (0, 0)))
+        src = jnp.pad(edge_source, (0, pad), constant_values=-1)[None, :]
+        valid = jnp.pad(edge_valid, (0, pad))[None, :]
         outgoing = jnp.einsum("sa,nac->nsc", send_hot, nodes, preferred_element_type=F32).astype(BF)
         incoming = [shifted(outgoing[:, i * halo : (i + 1) * halo], peer_steps[i]) for i in range(4)]
         table = jnp.concatenate([nodes, *incoming], axis=1)

time: 105 us -> 103 us (0.981)
  the two profiles are of different devices: /device:TPU:8 before, /device:TPU:0 now
where the time goes in v3:
time: 103 us
  Pallas kernels  90.3 us (88%)
  local copies, waits for them, and re-layouts  10.8 us (10%)
  other arithmetic  1.28 us (1%)
    pallas_call x1, Pallas kernels, fused(): pl.pallas_call(functools.partial(fused_kernel, neigh, ch, widths, graph),...  90.3 us
    unnamed x12, local copies, waits for them, and re-layouts  7.55 us

profile of v3, /device:TPU:0, one launch (start us, length us, event | category | flops | bytes accessed | tf_op | source)
XLA Modules:
  0.0 103.1 jit_solution(15114646838409131336)
XLA Ops:
  0.6 0.8 eq.22
  1.4 1.3 %broadcast_in_dim.7.src_ref = s32[1,576]{1,0:T(1,128)} reshape(s32[576]{0:T(1024)} %param.14) | data formatting | bytes 4608 | tf_op jit(solution)/shard_map/broadcast_in_dim | solution.py:637
  2.7 1.3 %broadcast_in_dim.8.valid_ref = s32[1,576]{1,0:T(1,128)} reshape(s32[576]{0:T(1024)} %param.15) | data formatting | bytes 4608 | tf_op jit(solution)/shard_map/broadcast_in_dim | solution.py:637
  3.9 0.7 fusion.1.sent_ref
  4.6 0.6 fusion.back_ref
  5.2 1.8 %copy.15.rot_ref = bf16[235,576]{1,0:T(8,128)(2,1)} copy(bf16[235,576]{0,1:T(8,128)(2,1)} %param.12) | data formatting | bytes 541440 | tf_op args[2]
  7.1 90.3 %fused.1 = (bf16[49,48,128]{2,1,0:T(8,128)(2,1)}, bf16[576,128]{1,0:T(8,128)(2,1)}, f32[392,128]{1,0:T(8,128)}, f32[576,128]{1,0:T(8,128)}, f32[400,128]{1,0:T(8,128)}) custom-call(bf16[49,48,128]{2,1,0:T(8,128)(2,1)} %bitcast.7, bf16[49,48,128]{2,1,0:T(8,128)(2,1)} %bitcast.8, bf16[235,576]{1,0:T(8,128)(2,1)} %copy.15.rot_ref, bf16[576,128]{1,0:T(8,128)(2,1)} %rad_ref.1, ...), custom_call_target="tpu_custom_call" | custom-call | tf_op jit(solution)/shard_map/fused/pallas_call | solution.py:550
  97.4 0.0 copy-start.2
  97.4 0.0 copy-start
  97.4 0.0 copy-start.1
  97.4 2.0 %copy.21 = bf16[48,49,128]{2,0,1:T(8,128)(2,1)} copy(bf16[48,49,128]{2,0,1:T(8,128)(2,1)} %bitcast.6) | data formatting | bytes 1204224
  99.4 1.6 %copy.22 = bf16[576,128]{1,0:T(8,128)(2,1)} copy(bf16[576,128]{1,0:T(8,128)(2,1)} %get-tuple-element.21) | data formatting | bytes 294912
  101.0 0.0 copy-done.2
  101.0 0.7 copy.23
  101.7 0.0 copy-done
  101.7 0.7 copy.24
  102.4 0.0 copy-done.1
  102.4 0.7 copy.25
Async XLA Ops:
  97.4 3.6 %copy-start.2 = (f32[392,128]{1,0:T(8,128)S(1)}, f32[392,128]{1,0:T(8,128)}, u32[]{:S(2)}) copy-start(f32[392,128]{1,0:T(8,128)} %get-tuple-element.12) | copy-start | bytes 602116
  97.4 4.3 %copy-start = (f32[576,128]{1,0:T(8,128)S(1)}, f32[576,128]{1,0:T(8,128)}, u32[]{:S(2)}) copy-start(f32[576,128]{1,0:T(8,128)} %get-tuple-element.13) | copy-start | bytes 884740
  97.4 5.0 %copy-start.1 = (f32[400,128]{1,0:T(8,128)S(1)}, f32[400,128]{1,0:T(8,128)}, u32[]{:S(2)}) copy-start(f32[400,128]{1,0:T(8,128)} %get-tuple-element.14) | copy-start | bytes 614404
